TPU v7x, 32 devices: a whole 2x2x4 slice. The times are simulated.
32 devices in a mesh: dp: 8 (over y, x, core), seq: 4 (over z).
Axes of the slice: x: 2, y: 2, z: 4, core: 2. Of those that a mesh axis runs over, the one named last changes fastest.
Arguments:
- tokens: bfloat16 [16, 640, 512], P('dp', 'seq'), may hold values from -6 to 6
- cotangent: bfloat16 [16, 640, 512], P('dp', 'seq'), may hold values from -6 to 6
- routes: int32 [2, 16, 640, 2], P(None, 'dp', 'seq'), may hold values from 0 to 3, all different within a row
- token_mask: int32 [16, 640], P('dp'), may hold values from 0 to 1, as said below
- ln1_gain: bfloat16 [2, 512], P(None, 'dp'), may hold values from 0.5 to 1.5
- ln1_bias: bfloat16 [2, 512], P(None, 'dp'), may hold values from -1.1953125 to 1.1953125
- qkv_weight: bfloat16 [2, 512, 1536], P(None, 'dp'), may hold values from -0.375 to 0.375
- out_weight: bfloat16 [2, 512, 512], P(None, 'dp'), may hold values from -1 to 1
- ln2_gain: bfloat16 [2, 512], P(None, 'dp'), may hold values from 0.5 to 1.5
- ln2_bias: bfloat16 [2, 512], P(None, 'dp'), may hold values from -1.1953125 to 1.1953125
- router_weight: bfloat16 [2, 512, 4], P(None, 'dp'), may hold values from -0.1875 to 0.1875
- expert_in: bfloat16 [2, 4, 512, 2048], P(None, None, 'dp'), may hold values from -0.25 to 0.25
- expert_out: bfloat16 [2, 4, 2048, 512], P(None, None, 'dp'), may hold values from -0.5 to 0.5
Outputs:
- output: bfloat16 [16, 640, 512], P('dp', 'seq')
- token_grad: float32 [16, 640, 512], P('dp', 'seq')
- ln1_gain_grad: float32 [2, 512], P(None, 'dp')
- ln1_bias_grad: float32 [2, 512], P(None, 'dp')
- qkv_weight_grad: float32 [2, 512, 1536], P(None, 'dp')
- out_weight_grad: float32 [2, 512, 512], P(None, 'dp')
- ln2_gain_grad: float32 [2, 512], P(None, 'dp')
- ln2_bias_grad: float32 [2, 512], P(None, 'dp')
- router_weight_grad: float32 [2, 512, 4], P(None, 'dp')
- expert_in_grad: float32 [2, 4, 512, 2048], P(None, None, 'dp')
- expert_out_grad: float32 [2, 4, 2048, 512], P(None, None, 'dp')
Inputs may be any that keep to these rules, and one draw needn't show every extreme that they name: `token_mask`: in each image the valid tokens (1) come first and the pads (0) after them; each image has 481 to 640 valid tokens. `routes`: the two experts of a token differ.
All inputs are finite; a program needn't handle non-finite values.
Results may differ from a plain program's by a relative error of at most 0.028.
Values may be sent and summed in bfloat16 or wider, within the bound.
A program may use at most 320 MiB of HBM per device.

v0:
```python
import jax
import jax.numpy as jnp
from jax import lax
from jax.sharding import PartitionSpec as P

HEAD = 64


EPS = 1e-06
NEG = -1e30
HIGH = lax.Precision.HIGHEST


def normalize(values):
    center = values - jnp.mean(values, -1, keepdims=True)
    inverse = lax.rsqrt(jnp.mean(center * center, -1, keepdims=True) + EPS)
    return (center * inverse, inverse)


def norm_back(grad_unit, unit, inverse):
    return inverse * (
        grad_unit
        - jnp.mean(grad_unit, -1, keepdims=True)
        - unit * jnp.mean(grad_unit * unit, -1, keepdims=True)
    )


def split_heads(values):
    batch, length, width = values.shape
    return values.reshape(batch, length, width // HEAD, HEAD)


def attention_scores(queries, keys_all, valid):
    scores = jnp.einsum(
        "bqhd,bkhd->bhqk",
        split_heads(queries),
        split_heads(keys_all),
        preferred_element_type=jnp.float32,
    ) * HEAD ** (-0.5)
    return jnp.where(valid[:, None, None, :] > 0, scores, NEG)


def gather_dense(level, dense):
    gain_one, bias_one, proj_packed, proj_out, gain_two, bias_two, router = (
        item[level] for item in dense
    )
    return (
        lax.all_gather(gain_one, "dp", axis=0, tiled=True),
        lax.all_gather(bias_one, "dp", axis=0, tiled=True),
        lax.all_gather(proj_packed, "dp", axis=0, tiled=True),
        lax.all_gather(proj_out, "dp", axis=0, tiled=True),
        lax.all_gather(gain_two, "dp", axis=0, tiled=True),
        lax.all_gather(bias_two, "dp", axis=0, tiled=True),
        lax.all_gather(router, "dp", axis=0, tiled=True),
    )


def hidden_of(normed_rows, rows_in):
    return jnp.dot(
        normed_rows,
        lax.all_gather(rows_in, "dp", axis=0, tiled=True),
        preferred_element_type=jnp.float32,
    )


def output_of(hidden_act, rows_out):
    return jnp.dot(
        hidden_act,
        lax.all_gather(rows_out, "dp", axis=0, tiled=True),
        preferred_element_type=jnp.float32,
    )


def gelu_exact(values):
    return jax.nn.gelu(values, approximate=False)


def shards(
    tokens,
    cotangent,
    routes,
    token_mask,
    ln1_gain,
    ln1_bias,
    qkv_weight,
    out_weight,
    ln2_gain,
    ln2_bias,
    router_weight,
    expert_in,
    expert_out,
):
    dense = (ln1_gain, ln1_bias, qkv_weight, out_weight, ln2_gain, ln2_bias, router_weight)
    images, local_len, width = tokens.shape
    levels = qkv_weight.shape[0]
    experts = expert_in.shape[1]
    tok_rows = images * local_len
    scale = HEAD ** (-0.5)
    offset = lax.axis_index("seq") * local_len
    local_valid = lax.dynamic_slice_in_dim(token_mask, offset, local_len, 1)
    state = tokens.astype(jnp.float32)
    saved = []
    for level in range(levels):
        gain_one, bias_one, proj_packed, proj_out, gain_two, bias_two, router = gather_dense(
            level, dense
        )
        unit_one, inverse_one = normalize(state)
        normed = (unit_one * gain_one + bias_one).astype(jnp.bfloat16)
        packed = jnp.einsum(
            "bld,de->ble", normed, proj_packed, preferred_element_type=jnp.float32
        ).astype(jnp.bfloat16)
        head_q, head_k, head_v = (
            lax.all_to_all(packed[..., :width], "seq", split_axis=2, concat_axis=1, tiled=True),
            lax.all_to_all(
                packed[..., width : 2 * width], "seq", split_axis=2, concat_axis=1, tiled=True
            ),
            lax.all_to_all(
                packed[..., 2 * width :], "seq", split_axis=2, concat_axis=1, tiled=True
            ),
        )
        scores = attention_scores(head_q, head_k, token_mask)
        highest = jnp.max(scores, -1, keepdims=True)
        expo = jnp.exp(scores - highest)
        totals = jnp.sum(expo, -1, keepdims=True)
        log_total = highest + jnp.log(totals)
        weights = (expo / totals).astype(jnp.bfloat16)
        mixed_heads = jnp.einsum(
            "bhqk,bkhd->bqhd", weights, split_heads(head_v), preferred_element_type=jnp.float32
        )
        mixed_heads = mixed_heads.reshape(head_q.shape).astype(jnp.bfloat16)
        mixed = lax.all_to_all(mixed_heads, "seq", split_axis=1, concat_axis=2, tiled=True)
        middle = state + jnp.einsum(
            "bld,de->ble", mixed, proj_out, preferred_element_type=jnp.float32
        )
        unit_two, inverse_two = normalize(middle)
        normed_two = (unit_two * gain_two + bias_two).astype(jnp.bfloat16).reshape(tok_rows, width)
        logits = jnp.dot(normed_two, router, preferred_element_type=jnp.float32)
        shifted = jnp.exp(logits - jnp.max(logits, -1, keepdims=True))
        gates = shifted / jnp.sum(shifted, -1, keepdims=True)
        route_rows = routes[level].reshape(tok_rows, 2)
        matches = route_rows[:, :, None] == jnp.arange(experts, dtype=jnp.int32)[None, None, :]
        chosen = jnp.sum(matches.astype(jnp.float32), 1)
        combine = gates * chosen
        update = jnp.zeros((tok_rows, width), jnp.float32)
        results = []
        hidden_keep = []
        weights_keep = []
        for expert in range(experts):
            hidden_pre = hidden_of(normed_two, expert_in[level, expert])
            hidden_act = gelu_exact(hidden_pre).astype(jnp.bfloat16)
            result = output_of(hidden_act, expert_out[level, expert])
            update = update + combine[:, expert : expert + 1] * result
            results.append(result)
        state = middle + update.reshape(images, local_len, width)
        saved.append(
            {
                "unit_one": unit_one,
                "inverse_one": inverse_one,
                "normed": normed,
                "head_q": head_q,
                "head_k": head_k,
                "head_v": head_v,
                "log_total": log_total,
                "mixed": mixed,
                "unit_two": unit_two,
                "inverse_two": inverse_two,
                "normed_two": normed_two,
                "gates": gates,
                "chosen": chosen,
                "combine": combine,
                "results": results,
                "hidden_keep": hidden_keep,
                "weights_keep": weights_keep,
            }
        )
    output = state.astype(jnp.bfloat16)
    grad = cotangent.astype(jnp.float32) * local_valid[..., None].astype(jnp.float32)
    layer_grads = [None] * levels
    for level in reversed(range(levels)):
        kept = saved[level]
        gain_one, bias_one, proj_packed, proj_out, gain_two, bias_two, router = gather_dense(
            level, dense
        )
        grad_rows = grad.reshape(tok_rows, width)
        normed_two = kept["normed_two"]
        gates = kept["gates"]
        chosen = kept["chosen"]
        combine = kept["combine"]
        grad_combine = jnp.stack(
            [jnp.sum(grad_rows * result, -1) for result in kept["results"]], -1
        )
        grad_gates = grad_combine * chosen
        grad_logits = gates * (grad_gates - jnp.sum(gates * grad_gates, -1, keepdims=True))
        grad_normed = jnp.dot(grad_logits, router.astype(jnp.float32).T, precision=HIGH)
        router_grad = jnp.dot(normed_two.astype(jnp.float32).T, grad_logits, precision=HIGH)
        up_list = []
        down_list = []
        for expert in range(experts):
            grad_result = (combine[:, expert : expert + 1] * grad_rows).astype(jnp.bfloat16)
            hidden_pre = hidden_of(normed_two, expert_in[level, expert])
            hidden_act = gelu_exact(hidden_pre).astype(jnp.bfloat16)
            grad_act = jnp.einsum(
                "td,hd->th",
                grad_result,
                lax.all_gather(expert_out[level, expert], "dp", axis=0, tiled=True),
                preferred_element_type=jnp.float32,
            )
            gelu_pull = jax.vjp(gelu_exact, hidden_pre)[1]
            grad_pre = gelu_pull(grad_act)[0].astype(jnp.bfloat16)
            grad_normed = grad_normed + jnp.einsum(
                "th,dh->td",
                grad_pre,
                lax.all_gather(expert_in[level, expert], "dp", axis=0, tiled=True),
                preferred_element_type=jnp.float32,
            )
            up_list.append(
                lax.psum_scatter(
                    jnp.einsum(
                        "td,th->dh", normed_two, grad_pre, preferred_element_type=jnp.float32
                    ).astype(jnp.bfloat16),
                    "dp",
                    scatter_dimension=0,
                    tiled=True,
                ).astype(jnp.float32)
            )
            down_list.append(
                lax.psum_scatter(
                    jnp.einsum(
                        "th,td->hd", hidden_act, grad_result, preferred_element_type=jnp.float32
                    ).astype(jnp.bfloat16),
                    "dp",
                    scatter_dimension=0,
                    tiled=True,
                ).astype(jnp.float32)
            )
        grad_normed = grad_normed.reshape(images, local_len, width)
        unit_two = kept["unit_two"]
        gain_two_grad = jnp.sum(grad_normed * unit_two, (0, 1))
        bias_two_grad = jnp.sum(grad_normed, (0, 1))
        grad_middle = grad + norm_back(grad_normed * gain_two, unit_two, kept["inverse_two"])
        grad_branch = grad_middle.astype(jnp.bfloat16)
        out_grad = jnp.einsum(
            "bld,ble->de", kept["mixed"], grad_branch, preferred_element_type=jnp.float32
        )
        grad_mixed = jnp.einsum(
            "ble,de->bld", grad_branch, proj_out, preferred_element_type=jnp.float32
        ).astype(jnp.bfloat16)
        grad_heads = lax.all_to_all(grad_mixed, "seq", split_axis=2, concat_axis=1, tiled=True)
        head_q = kept["head_q"]
        head_k = kept["head_k"]
        head_v = kept["head_v"]
        scores = attention_scores(head_q, head_k, token_mask)
        probs = jnp.exp(scores - kept["log_total"])
        grad_split = split_heads(grad_heads)
        grad_v = jnp.einsum(
            "bhqk,bqhd->bkhd",
            probs.astype(jnp.bfloat16),
            grad_split,
            preferred_element_type=jnp.float32,
        )
        grad_probs = jnp.einsum(
            "bqhd,bkhd->bhqk", grad_split, split_heads(head_v), preferred_element_type=jnp.float32
        )
        grad_scores = (
            probs * (grad_probs - jnp.sum(probs * grad_probs, -1, keepdims=True))
        ).astype(jnp.bfloat16)
        grad_q = scale * jnp.einsum(
            "bhqk,bkhd->bqhd", grad_scores, split_heads(head_k), preferred_element_type=jnp.float32
        )
        grad_k = scale * jnp.einsum(
            "bhqk,bqhd->bkhd", grad_scores, split_heads(head_q), preferred_element_type=jnp.float32
        )
        head_shape = head_q.shape
        grad_q_tok, grad_k_tok, grad_v_tok = (
            lax.all_to_all(
                grad_q.reshape(head_shape).astype(jnp.bfloat16),
                "seq",
                split_axis=1,
                concat_axis=2,
                tiled=True,
            ),
            lax.all_to_all(
                grad_k.reshape(head_shape).astype(jnp.bfloat16),
                "seq",
                split_axis=1,
                concat_axis=2,
                tiled=True,
            ),
            lax.all_to_all(
                grad_v.reshape(head_shape).astype(jnp.bfloat16),
                "seq",
                split_axis=1,
                concat_axis=2,
                tiled=True,
            ),
        )
        grad_packed = jnp.concatenate([grad_q_tok, grad_k_tok, grad_v_tok], -1)
        grad_normed_one = jnp.einsum(
            "ble,de->bld", grad_packed, proj_packed, preferred_element_type=jnp.float32
        )
        packed_grad = jnp.einsum(
            "bld,ble->de", kept["normed"], grad_packed, preferred_element_type=jnp.float32
        )
        unit_one = kept["unit_one"]
        gain_one_grad = jnp.sum(grad_normed_one * unit_one, (0, 1))
        bias_one_grad = jnp.sum(grad_normed_one, (0, 1))
        grad = grad_middle + norm_back(grad_normed_one * gain_one, unit_one, kept["inverse_one"])
        shares = (
            lax.psum_scatter(
                gain_one_grad.astype(jnp.bfloat16), "dp", scatter_dimension=0, tiled=True
            ).astype(jnp.float32),
            lax.psum_scatter(
                bias_one_grad.astype(jnp.bfloat16), "dp", scatter_dimension=0, tiled=True
            ).astype(jnp.float32),
            lax.psum_scatter(
                packed_grad.astype(jnp.bfloat16), "dp", scatter_dimension=0, tiled=True
            ).astype(jnp.float32),
            lax.psum_scatter(
                out_grad.astype(jnp.bfloat16), "dp", scatter_dimension=0, tiled=True
            ).astype(jnp.float32),
            lax.psum_scatter(
                gain_two_grad.astype(jnp.bfloat16), "dp", scatter_dimension=0, tiled=True
            ).astype(jnp.float32),
            lax.psum_scatter(
                bias_two_grad.astype(jnp.bfloat16), "dp", scatter_dimension=0, tiled=True
            ).astype(jnp.float32),
            lax.psum_scatter(
                router_grad.astype(jnp.bfloat16), "dp", scatter_dimension=0, tiled=True
            ).astype(jnp.float32),
        )
        layer_grads[level] = (
            lax.psum(shares[0].astype(jnp.bfloat16), "seq").astype(jnp.float32),
            lax.psum(shares[1].astype(jnp.bfloat16), "seq").astype(jnp.float32),
            lax.psum(shares[2].astype(jnp.bfloat16), "seq").astype(jnp.float32),
            lax.psum(shares[3].astype(jnp.bfloat16), "seq").astype(jnp.float32),
            lax.psum(shares[4].astype(jnp.bfloat16), "seq").astype(jnp.float32),
            lax.psum(shares[5].astype(jnp.bfloat16), "seq").astype(jnp.float32),
            lax.psum(shares[6].astype(jnp.bfloat16), "seq").astype(jnp.float32),
            lax.psum(jnp.stack(up_list).astype(jnp.bfloat16), "seq").astype(jnp.float32),
            lax.psum(jnp.stack(down_list).astype(jnp.bfloat16), "seq").astype(jnp.float32),
        )
    stacked = [
        jnp.stack([layer_grads[level][kind] for level in range(levels)]) for kind in range(9)
    ]
    return (
        output,
        grad,
        stacked[0],
        stacked[1],
        stacked[2],
        stacked[3],
        stacked[4],
        stacked[5],
        stacked[6],
        stacked[7],
        stacked[8],
    )


def solution(mesh):
    return jax.shard_map(
        shards,
        mesh=mesh,
        in_specs=(
            P("dp", "seq", None),
            P("dp", "seq", None),
            P(None, "dp", "seq", None),
            P("dp", None),
            P(None, "dp"),
            P(None, "dp"),
            P(None, "dp", None),
            P(None, "dp", None),
            P(None, "dp"),
            P(None, "dp"),
            P(None, "dp", None),
            P(None, None, "dp", None),
            P(None, None, "dp", None),
        ),
        out_specs=(
            P("dp", "seq", None),
            P("dp", "seq", None),
            P(None, "dp"),
            P(None, "dp"),
            P(None, "dp", None),
            P(None, "dp", None),
            P(None, "dp"),
            P(None, "dp"),
            P(None, "dp", None),
            P(None, None, "dp", None),
            P(None, None, "dp", None),
        ),
        check_vma=False,
    )
```

profile of v0, /device:TPU:0, one launch (start us, length us, event | category | flops | bytes accessed | tf_op | source)
XLA Modules:
  0.0 1700.2 jit_solution(14331543530220702980)
XLA Ops:
  25.5 16.1 all-reduce.17
  52.2 11.6 all-to-all-done.2
  68.4 11.2 all-to-all-done.1
  85.7 9.5 all-to-all-done
  106.5 12.8 all-gather.6
  119.5 11.7 all-gather.3
  133.2 9.7 multiply_convert_fusion.6
  151.7 10.0 multiply_convert_fusion.8
  161.7 9.5 multiply_convert_fusion.9
  171.2 20.1 %all-gather.61.cloned.1.call-done = bf16[1,1,2048,512]{3,2,1,0:T(8,128)(2,1)} async-done(((bf16[1,1,256,512]{3,2,1,0:T(8,128)(2,1)}), bf16[1,1,2048,512]{3,2,1,0:T(8,128)(2,1)}) %all-gather.61.cloned.1.call-update) | async-done | bytes 2097168 | tf_op jit(solution)/shard_map/all_gather | solution.py:69
  193.7 27.4 %all-gather.57.cloned.1.call-done = bf16[1,1,2048,512]{3,2,1,0:T(8,128)(2,1)} async-done(((bf16[1,1,256,512]{3,2,1,0:T(8,128)(2,1)}), bf16[1,1,2048,512]{3,2,1,0:T(8,128)(2,1)}) %all-gather.57.cloned.1.call-update) | async-done | bytes 2097168 | tf_op jit(solution)/shard_map/all_gather | solution.py:69
  224.0 26.9 %all-gather.53.cloned.1.call-done = bf16[1,1,2048,512]{3,2,1,0:T(8,128)(2,1)} async-done(((bf16[1,1,256,512]{3,2,1,0:T(8,128)(2,1)}), bf16[1,1,2048,512]{3,2,1,0:T(8,128)(2,1)}) %all-gather.53.cloned.1.call-update) | async-done | bytes 2097168 | tf_op jit(solution)/shard_map/all_gather | solution.py:69
  253.8 27.0 %all-gather.65.cloned.1.call-done = bf16[1,1,2048,512]{3,2,1,0:T(8,128)(2,1)} async-done(((bf16[1,1,256,512]{3,2,1,0:T(8,128)(2,1)}), bf16[1,1,2048,512]{3,2,1,0:T(8,128)(2,1)}) %all-gather.65.cloned.1.call-update) | async-done | bytes 2097168 | tf_op jit(solution)/shard_map/all_gather | solution.py:69
  284.9 23.3 %all-gather.67.cloned.1.call-done = bf16[1,512,1536]{2,1,0:T(8,128)(2,1)} async-done(((bf16[1,64,1536]{2,1,0:T(8,128)(2,1)}), bf16[1,512,1536]{2,1,0:T(8,128)(2,1)}) %all-gather.67.cloned.1.call-update) | async-done | bytes 1572880 | tf_op jit(solution)/shard_map/all_gather | solution.py:50
  317.2 13.8 all-to-all-done.6
  335.8 13.0 all-to-all-done.5
  354.4 11.9 all-to-all-done.4
  378.3 9.3 all-gather.21
  387.8 11.3 all-gather.18
  401.0 9.5 multiply_convert_fusion.2
  410.5 9.6 multiply_convert_fusion.3
  432.0 26.8 %all-gather.73.cloned.1.call-done = bf16[1,1,512,2048]{3,2,1,0:T(8,128)(2,1)} async-done(((bf16[1,1,64,2048]{3,2,1,0:T(8,128)(2,1)}), bf16[1,1,512,2048]{3,2,1,0:T(8,128)(2,1)}) %all-gather.73.cloned.1.call-update) | async-done | bytes 2097168 | tf_op jit(solution)/shard_map/all_gather | solution.py:61
  458.8 9.5 multiply_convert_fusion.4
  468.3 20.2 %all-gather.75.cloned.1.call-done = bf16[1,1,2048,512]{3,2,1,0:T(8,128)(2,1)} async-done(((bf16[1,1,256,512]{3,2,1,0:T(8,128)(2,1)}), bf16[1,1,2048,512]{3,2,1,0:T(8,128)(2,1)}) %all-gather.75.cloned.1.call-update) | async-done | bytes 2097168 | tf_op jit(solution)/shard_map/all_gather | solution.py:69
  491.3 27.4 %all-gather.69.cloned.1.call-done = bf16[1,1,512,2048]{3,2,1,0:T(8,128)(2,1)} async-done(((bf16[1,1,64,2048]{3,2,1,0:T(8,128)(2,1)}), bf16[1,1,512,2048]{3,2,1,0:T(8,128)(2,1)}) %all-gather.69.cloned.1.call-update) | async-done | bytes 2097168 | tf_op jit(solution)/shard_map/all_gather | solution.py:61
  518.7 9.7 multiply_convert_fusion.5
  528.4 20.0 %all-gather.71.cloned.1.call-done = bf16[1,1,2048,512]{3,2,1,0:T(8,128)(2,1)} async-done(((bf16[1,1,256,512]{3,2,1,0:T(8,128)(2,1)}), bf16[1,1,2048,512]{3,2,1,0:T(8,128)(2,1)}) %all-gather.71.cloned.1.call-update) | async-done | bytes 2097168 | tf_op jit(solution)/shard_map/all_gather | solution.py:69
  612.7 10.9 all-to-all-done.8
  747.5 9.8 all-to-all-done.12
  824.9 44.6 %reduce-scatter.63.cloned.1.call-done = bf16[256,512]{1,0:T(8,128)(2,1)} async-done(((bf16[2048,512]{1,0:T(8,128)(2,1)}), bf16[256,512]{1,0:T(8,128)(2,1)}) %reduce-scatter.63.cloned.1.call-update) | async-done | bytes 262160 | tf_op jit(solution)/shard_map/reduce_scatter | solution.py:227
  869.4 44.8 %reduce-scatter.65.cloned.1.call-done = bf16[256,512]{1,0:T(8,128)(2,1)} async-done(((bf16[2048,512]{1,0:T(8,128)(2,1)}), bf16[256,512]{1,0:T(8,128)(2,1)}) %reduce-scatter.65.cloned.1.call-update) | async-done | bytes 262160 | tf_op jit(solution)/shard_map/reduce_scatter | solution.py:227
  916.5 42.1 %reduce-scatter.35.cloned.1.call-done = bf16[64,2048]{1,0:T(8,128)(2,1)} async-done(((bf16[512,2048]{1,0:T(8,128)(2,1)}), bf16[64,2048]{1,0:T(8,128)(2,1)}) %reduce-scatter.35.cloned.1.call-update) | async-done | bytes 262160 | tf_op jit(solution)/shard_map/reduce_scatter | solution.py:217
  958.6 44.9 %reduce-scatter.37.cloned.1.call-done = bf16[64,2048]{1,0:T(8,128)(2,1)} async-done(((bf16[512,2048]{1,0:T(8,128)(2,1)}), bf16[64,2048]{1,0:T(8,128)(2,1)}) %reduce-scatter.37.cloned.1.call-update) | async-done | bytes 262160 | tf_op jit(solution)/shard_map/reduce_scatter | solution.py:217
  1003.5 45.1 %reduce-scatter.39.cloned.1.call-done = bf16[64,2048]{1,0:T(8,128)(2,1)} async-done(((bf16[512,2048]{1,0:T(8,128)(2,1)}), bf16[64,2048]{1,0:T(8,128)(2,1)}) %reduce-scatter.39.cloned.1.call-update) | async-done | bytes 262160 | tf_op jit(solution)/shard_map/reduce_scatter | solution.py:217
  1048.6 45.3 %reduce-scatter.41.cloned.1.call-done = bf16[64,2048]{1,0:T(8,128)(2,1)} async-done(((bf16[512,2048]{1,0:T(8,128)(2,1)}), bf16[64,2048]{1,0:T(8,128)(2,1)}) %reduce-scatter.41.cloned.1.call-update) | async-done | bytes 262160 | tf_op jit(solution)/shard_map/reduce_scatter | solution.py:217
  1096.2 42.3 %reduce-scatter.51.cloned.1.call-done = bf16[256,512]{1,0:T(8,128)(2,1)} async-done(((bf16[2048,512]{1,0:T(8,128)(2,1)}), bf16[256,512]{1,0:T(8,128)(2,1)}) %reduce-scatter.51.cloned.1.call-update) | async-done | bytes 262160 | tf_op jit(solution)/shard_map/reduce_scatter | solution.py:227
  1138.5 44.9 %reduce-scatter.53.cloned.1.call-done = bf16[256,512]{1,0:T(8,128)(2,1)} async-done(((bf16[2048,512]{1,0:T(8,128)(2,1)}), bf16[256,512]{1,0:T(8,128)(2,1)}) %reduce-scatter.53.cloned.1.call-update) | async-done | bytes 262160 | tf_op jit(solution)/shard_map/reduce_scatter | solution.py:227
  1183.4 44.4 %reduce-scatter.55.cloned.1.call-done = bf16[256,512]{1,0:T(8,128)(2,1)} async-done(((bf16[2048,512]{1,0:T(8,128)(2,1)}), bf16[256,512]{1,0:T(8,128)(2,1)}) %reduce-scatter.55.cloned.1.call-update) | async-done | bytes 262160 | tf_op jit(solution)/shard_map/reduce_scatter | solution.py:227
  1227.8 44.9 %reduce-scatter.57.cloned.1.call-done = bf16[256,512]{1,0:T(8,128)(2,1)} async-done(((bf16[2048,512]{1,0:T(8,128)(2,1)}), bf16[256,512]{1,0:T(8,128)(2,1)}) %reduce-scatter.57.cloned.1.call-update) | async-done | bytes 262160 | tf_op jit(solution)/shard_map/reduce_scatter | solution.py:227
  1275.0 34.9 %reduce-scatter.33.cloned.1.call-done = bf16[64,512]{1,0:T(8,128)(2,1)} async-done(((bf16[512,512]{1,0:T(8,128)(2,1)}), bf16[64,512]{1,0:T(8,128)(2,1)}) %reduce-scatter.33.cloned.1.call-update) | async-done | bytes 65552 | tf_op jit(solution)/shard_map/reduce_scatter | solution.py:318
  1309.9 37.4 %reduce-scatter.31.cloned.1.call-done = bf16[64,512]{1,0:T(8,128)(2,1)} async-done(((bf16[512,512]{1,0:T(8,128)(2,1)}), bf16[64,512]{1,0:T(8,128)(2,1)}) %reduce-scatter.31.cloned.1.call-update) | async-done | bytes 65552 | tf_op jit(solution)/shard_map/reduce_scatter | solution.py:318
  1347.3 41.6 %reduce-scatter.29.cloned.1.call-done = bf16[64,1536]{1,0:T(8,128)(2,1)} async-done(((bf16[512,1536]{1,0:T(8,128)(2,1)}), bf16[64,1536]{1,0:T(8,128)(2,1)}) %reduce-scatter.29.cloned.1.call-update) | async-done | bytes 196624 | tf_op jit(solution)/shard_map/reduce_scatter | solution.py:315
  1388.9 41.8 %reduce-scatter.27.cloned.1.call-done = bf16[64,1536]{1,0:T(8,128)(2,1)} async-done(((bf16[512,1536]{1,0:T(8,128)(2,1)}), bf16[64,1536]{1,0:T(8,128)(2,1)}) %reduce-scatter.27.cloned.1.call-update) | async-done | bytes 196624 | tf_op jit(solution)/shard_map/reduce_scatter | solution.py:315
  1431.5 36.0 %reduce-scatter.69.cloned.1.call-done = bf16[64,4]{1,0:T(8,128)(2,1)} async-done(((bf16[512,4]{1,0:T(8,128)(2,1)}), bf16[64,4]{1,0:T(8,128)(2,1)}) %reduce-scatter.69.cloned.1.call-update) | async-done | bytes 528
  1468.3 36.5 %reduce-scatter.67.cloned.1.call-done = bf16[64,4]{1,0:T(8,128)(2,1)} async-done(((bf16[512,4]{1,0:T(8,128)(2,1)}), bf16[64,4]{1,0:T(8,128)(2,1)}) %reduce-scatter.67.cloned.1.call-update) | async-done | bytes 528
  1507.9 12.5 all-reduce.16
  1521.0 12.8 all-reduce.18
  1537.8 145.3 %all-reduce.22.cloned.1.call-done = (bf16[1,64,1536]{2,1,0:T(8,128)(2,1)}, bf16[1,64,1536]{2,1,0:T(8,128)(2,1)}, bf16[1,64,512]{2,1,0:T(8,128)(2,1)}, bf16[1,64,...) async-done(((bf16[1,64,1536]{2,1,0:T(8,128)(2,1)}, ...) | async-done | bytes 4718608 | tf_op jit(solution)/shard_map/psum | solution.py:334
  (680 shorter events, 399.9 us)
Async XLA Ops:
  7.2 35.0 %all-gather.49.cloned.1.call-start = ((), (), s32[]{:S(2)}) async-start(), calls=%async_computation.58 | async-start | bytes 1769472 | tf_op jit(solution)/shard_map/all_gather | solution.py:50
  9.0 124.2 %all-gather.63.cloned.1.call-start = ((), (), s32[]{:S(2)}) async-start(), calls=%async_computation.65 | async-start | bytes 2359296 | tf_op jit(solution)/shard_map/all_gather | solution.py:61
  12.1 130.8 %all-gather.59.cloned.1.call-start = ((), (), s32[]{:S(2)}) async-start(), calls=%async_computation.63 | async-start | bytes 2359296 | tf_op jit(solution)/shard_map/all_gather | solution.py:61
  12.8 138.9 %all-gather.55.cloned.1.call-start = ((), (), s32[]{:S(2)}) async-start(), calls=%async_computation.61 | async-start | bytes 2359296 | tf_op jit(solution)/shard_map/all_gather | solution.py:61
  13.4 148.3 %all-gather.51.cloned.1.call-start = ((), (), s32[]{:S(2)}) async-start(), calls=%async_computation.59 | async-start | bytes 2359296 | tf_op jit(solution)/shard_map/all_gather | solution.py:61
  14.1 177.2 %all-gather.61.cloned.1.call-start = ((), (), s32[]{:S(2)}) async-start(), calls=%async_computation.64 | async-start | bytes 2359296 | tf_op jit(solution)/shard_map/all_gather | solution.py:69
  15.7 205.4 %all-gather.57.cloned.1.call-start = ((), (), s32[]{:S(2)}) async-start(), calls=%async_computation.62 | async-start | bytes 2359296 | tf_op jit(solution)/shard_map/all_gather | solution.py:69
  16.4 234.5 %all-gather.53.cloned.1.call-start = ((), (), s32[]{:S(2)}) async-start(), calls=%async_computation.60 | async-start | bytes 2359296 | tf_op jit(solution)/shard_map/all_gather | solution.py:69
  17.2 263.6 %all-gather.65.cloned.1.call-start = ((), (), s32[]{:S(2)}) async-start(), calls=%async_computation.66 | async-start | bytes 2359296 | tf_op jit(solution)/shard_map/all_gather | solution.py:69
  17.9 290.3 %all-gather.67.cloned.1.call-start = ((), (), s32[]{:S(2)}) async-start(), calls=%async_computation.67 | async-start | bytes 1769472 | tf_op jit(solution)/shard_map/all_gather | solution.py:50
  18.5 382.5 %all-gather.81.cloned.1.call-start = ((), (), s32[]{:S(2)}) async-start(), calls=%async_computation.74 | async-start | bytes 2359296 | tf_op jit(solution)/shard_map/all_gather | solution.py:61
  19.2 391.3 %all-gather.77.cloned.1.call-start = ((), (), s32[]{:S(2)}) async-start(), calls=%async_computation.72 | async-start | bytes 2359296 | tf_op jit(solution)/shard_map/all_gather | solution.py:61
  19.8 400.4 %all-gather.83.cloned.1.call-start = ((), (), s32[]{:S(2)}) async-start(), calls=%async_computation.75 | async-start | bytes 2359296 | tf_op jit(solution)/shard_map/all_gather | solution.py:69
  20.5 408.6 %all-gather.79.cloned.1.call-start = ((), (), s32[]{:S(2)}) async-start(), calls=%async_computation.73 | async-start | bytes 2359296 | tf_op jit(solution)/shard_map/all_gather | solution.py:69
  21.1 437.7 %all-gather.73.cloned.1.call-start = ((), (), s32[]{:S(2)}) async-start(), calls=%async_computation.70 | async-start | bytes 2359296 | tf_op jit(solution)/shard_map/all_gather | solution.py:61
  21.7 466.7 %all-gather.75.cloned.1.call-start = ((), (), s32[]{:S(2)}) async-start(), calls=%async_computation.71 | async-start | bytes 2359296 | tf_op jit(solution)/shard_map/all_gather | solution.py:69
  46.1 17.7 %all-to-all-start.2 = ((bf16[2,160,512]{1,0,2:T(2,128)(2,1)}), bf16[2,160,512]{1,0,2:T(2,128)(2,1)S(1)}, u32[]{:S(2)}, u32[]{:S(2)}) async-start(bf16[2,160,512]{1,0,2:T(2,128)(2,1)} %copy.198), calls=%async_computation.2 | async-start | bytes 1048576 | tf_op jit(solution)/shard_map/all_to_all | solution.py:114
  83.0 435.7 %all-gather.69.cloned.1.call-start = ((), (), s32[]{:S(2)}) async-start(), calls=%async_computation.68 | async-start | bytes 2359296 | tf_op jit(solution)/shard_map/all_gather | solution.py:61
  102.7 28.5 %all-to-all-start.3 = ((bf16[2,640,128]{2,0,1:T(2,128)(2,1)}), bf16[2,640,128]{2,0,1:T(2,128)(2,1)S(1)}, u32[]{:S(2)}, u32[]{:S(2)}) async-start(bf16[2,640,128]{2,0,1:T(2,128)(2,1)} %copy.201), calls=%async_computation.3 | async-start | bytes 655360 | tf_op jit(solution)/shard_map/all_to_all | solution.py:131
  311.5 19.5 %all-to-all-start.6 = ((bf16[2,160,512]{1,0,2:T(2,128)(2,1)}), bf16[2,160,512]{1,0,2:T(2,128)(2,1)S(1)}, u32[]{:S(2)}, u32[]{:S(2)}) async-start(bf16[2,160,512]{1,0,2:T(2,128)(2,1)} %copy.211), calls=%async_computation.6 | async-start | bytes 1048576 | tf_op jit(solution)/shard_map/all_to_all | solution.py:114
  331.1 17.7 %all-to-all-start.5 = ((bf16[2,160,512]{1,0,2:T(2,128)(2,1)}), bf16[2,160,512]{1,0,2:T(2,128)(2,1)S(1)}, u32[]{:S(2)}, u32[]{:S(2)}) async-start(bf16[2,160,512]{1,0,2:T(2,128)(2,1)} %copy.209), calls=%async_computation.5 | async-start | bytes 1048576 | tf_op jit(solution)/shard_map/all_to_all | solution.py:113
  348.8 17.4 %all-to-all-start.4 = ((bf16[2,160,512]{1,0,2:T(2,128)(2,1)}), bf16[2,160,512]{1,0,2:T(2,128)(2,1)S(1)}, u32[]{:S(2)}, u32[]{:S(2)}) async-start(bf16[2,160,512]{1,0,2:T(2,128)(2,1)} %copy.207), calls=%async_computation.4 | async-start | bytes 1048576 | tf_op jit(solution)/shard_map/all_to_all | solution.py:117
  352.3 196.1 %all-gather.71.cloned.1.call-start = ((), (), s32[]{:S(2)}) async-start(), calls=%async_computation.69 | async-start | bytes 2359296 | tf_op jit(solution)/shard_map/all_gather | solution.py:69
  373.8 25.4 %all-to-all-start.7 = ((bf16[2,640,128]{2,0,1:T(2,128)(2,1)}), bf16[2,640,128]{2,0,1:T(2,128)(2,1)S(1)}, u32[]{:S(2)}, u32[]{:S(2)}) async-start(bf16[2,640,128]{2,0,1:T(2,128)(2,1)} %copy.214), calls=%async_computation.7 | async-start | bytes 655360 | tf_op jit(solution)/shard_map/all_to_all | solution.py:131
  377.3 436.0 %reduce-scatter.43.cloned.1.call-start = ((), (), s32[]{:S(2)}) async-start(), calls=%async_computation.46 | async-start | bytes 2359296 | tf_op jit(solution)/shard_map/reduce_scatter | solution.py:217
  559.9 253.3 %reduce-scatter.45.cloned.1.call-start = ((), (), s32[]{:S(2)}) async-start(), calls=%async_computation.47 | async-start | bytes 2359296 | tf_op jit(solution)/shard_map/reduce_scatter | solution.py:217
  568.3 245.0 %reduce-scatter.47.cloned.1.call-start = ((), (), s32[]{:S(2)}) async-start(), calls=%async_computation.48 | async-start | bytes 2359296 | tf_op jit(solution)/shard_map/reduce_scatter | solution.py:217
  577.2 236.1 %reduce-scatter.49.cloned.1.call-start = ((), (), s32[]{:S(2)}) async-start(), calls=%async_computation.49 | async-start | bytes 2359296 | tf_op jit(solution)/shard_map/reduce_scatter | solution.py:217
  585.6 230.1 %reduce-scatter.59.cloned.1.call-start = ((), (), s32[]{:S(2)}) async-start(), calls=%async_computation.54 | async-start | bytes 2359296 | tf_op jit(solution)/shard_map/reduce_scatter | solution.py:227
  588.3 236.5 %reduce-scatter.61.cloned.1.call-start = ((), (), s32[]{:S(2)}) async-start(), calls=%async_computation.55 | async-start | bytes 2359296 | tf_op jit(solution)/shard_map/reduce_scatter | solution.py:227
  604.0 19.5 %all-to-all-start.8 = ((bf16[2,160,512]{1,0,2:T(2,128)(2,1)}), bf16[2,160,512]{1,0,2:T(2,128)(2,1)S(1)}, u32[]{:S(2)}, u32[]{:S(2)}) async-start(bf16[2,160,512]{1,0,2:T(2,128)(2,1)} %copy.220), calls=%async_computation.8 | async-start | bytes 1048576 | tf_op jit(solution)/shard_map/all_to_all | solution.py:248
  608.6 260.9 %reduce-scatter.63.cloned.1.call-start = ((), (), s32[]{:S(2)}) async-start(), calls=%async_computation.56 | async-start | bytes 2359296 | tf_op jit(solution)/shard_map/reduce_scatter | solution.py:227
  662.3 251.9 %reduce-scatter.65.cloned.1.call-start = ((), (), s32[]{:S(2)}) async-start(), calls=%async_computation.57 | async-start | bytes 2359296 | tf_op jit(solution)/shard_map/reduce_scatter | solution.py:227
  666.3 292.3 %reduce-scatter.35.cloned.1.call-start = ((), (), s32[]{:S(2)}) async-start(), calls=%async_computation.42 | async-start | bytes 2359296 | tf_op jit(solution)/shard_map/reduce_scatter | solution.py:217
  681.7 321.8 %reduce-scatter.37.cloned.1.call-start = ((), (), s32[]{:S(2)}) async-start(), calls=%async_computation.43 | async-start | bytes 2359296 | tf_op jit(solution)/shard_map/reduce_scatter | solution.py:217
  690.0 358.6 %reduce-scatter.39.cloned.1.call-start = ((), (), s32[]{:S(2)}) async-start(), calls=%async_computation.44 | async-start | bytes 2359296 | tf_op jit(solution)/shard_map/reduce_scatter | solution.py:217
  698.7 395.3 %reduce-scatter.41.cloned.1.call-start = ((), (), s32[]{:S(2)}) async-start(), calls=%async_computation.45 | async-start | bytes 2359296 | tf_op jit(solution)/shard_map/reduce_scatter | solution.py:217
  707.3 431.1 %reduce-scatter.51.cloned.1.call-start = ((), (), s32[]{:S(2)}) async-start(), calls=%async_computation.50 | async-start | bytes 2359296 | tf_op jit(solution)/shard_map/reduce_scatter | solution.py:227
  711.4 472.0 %reduce-scatter.53.cloned.1.call-start = ((), (), s32[]{:S(2)}) async-start(), calls=%async_computation.51 | async-start | bytes 2359296 | tf_op jit(solution)/shard_map/reduce_scatter | solution.py:227
  715.4 512.4 %reduce-scatter.55.cloned.1.call-start = ((), (), s32[]{:S(2)}) async-start(), calls=%async_computation.52 | async-start | bytes 2359296 | tf_op jit(solution)/shard_map/reduce_scatter | solution.py:227
  719.4 553.2 %reduce-scatter.57.cloned.1.call-start = ((), (), s32[]{:S(2)}) async-start(), calls=%async_computation.53 | async-start | bytes 2359296 | tf_op jit(solution)/shard_map/reduce_scatter | solution.py:227
  723.6 586.3 %reduce-scatter.33.cloned.1.call-start = ((), (), s32[]{:S(2)}) async-start(), calls=%async_computation.41 | async-start | bytes 589824 | tf_op jit(solution)/shard_map/reduce_scatter | solution.py:318
  724.9 622.4 %reduce-scatter.31.cloned.1.call-start = ((), (), s32[]{:S(2)}) async-start(), calls=%async_computation.40 | async-start | bytes 589824 | tf_op jit(solution)/shard_map/reduce_scatter | solution.py:318
  745.1 643.9 %reduce-scatter.29.cloned.1.call-start = ((), (), s32[]{:S(2)}) async-start(), calls=%async_computation.39 | async-start | bytes 1769472 | tf_op jit(solution)/shard_map/reduce_scatter | solution.py:315
  800.9 629.8 %reduce-scatter.27.cloned.1.call-start = ((), (), s32[]{:S(2)}) async-start(), calls=%async_computation.38 | async-start | bytes 1769472 | tf_op jit(solution)/shard_map/reduce_scatter | solution.py:315
  810.8 656.7 %reduce-scatter.69.cloned.1.call-start = ((), (), s32[]{:S(2)}) async-start(), calls=%async_computation.77 | async-start | bytes 147456
  812.0 692.8 %reduce-scatter.67.cloned.1.call-start = ((), (), s32[]{:S(2)}) async-start(), calls=%async_computation.76 | async-start | bytes 147456
  813.2 870.0 %all-reduce.22.cloned.1.call-start = ((), (), s32[]{:S(2)}) async-start(), calls=%async_computation.78 | async-start | bytes 9437184 | tf_op jit(solution)/shard_map/psum | solution.py:334
  (164 other events, 2487.8 us)
Sparse Core Ops, SparseCore 0:
  10.5 28.6 all-gather.48
  41.6 27.9 all-gather.62
  72.1 27.8 all-gather.58
  101.7 30.1 all-gather.54
  133.7 27.9 all-gather.50
  163.4 27.8 all-gather.60
  193.2 27.8 all-gather.56
  223.0 27.8 all-gather.52
  252.8 27.8 all-gather.64
  282.5 25.6 all-gather.66
  310.1 27.8 all-gather.80
  339.8 27.8 all-gather.76
  369.6 30.0 all-gather.82
  401.4 27.6 all-gather.78
  430.8 27.8 all-gather.72
  460.5 27.8 all-gather.74
  490.8 27.8 all-gather.68
  520.4 27.8 all-gather.70
  560.1 41.2 reduce-scatter.42
  604.8 41.2 reduce-scatter.44
  649.4 41.1 reduce-scatter.46
  694.3 41.2 reduce-scatter.48
  738.8 41.2 reduce-scatter.58
  783.6 41.2 reduce-scatter.60
  828.2 41.2 reduce-scatter.62
  872.9 41.2 reduce-scatter.64
  917.3 41.2 reduce-scatter.34
  962.2 41.2 reduce-scatter.36
  1007.4 41.2 reduce-scatter.38
  1052.7 41.2 reduce-scatter.40
  1097.2 41.2 reduce-scatter.50
  1142.1 41.2 reduce-scatter.52
  1186.5 41.2 reduce-scatter.54
  1231.4 41.2 reduce-scatter.56
  1275.8 34.1 reduce-scatter.32
  1313.1 34.1 reduce-scatter.30
  1350.5 38.4 reduce-scatter.28
  1392.2 38.4 reduce-scatter.26
  1434.2 33.3 reduce-scatter.68
  1471.4 33.3 reduce-scatter.66
  1508.3 174.7 all-reduce.21
where the time goes:
time: 1710 us; the launch traced here: 1700 us
  waiting for transfers between devices  1170 us (68%)
  matrix products  246 us (14%)
  blocking collectives  86.5 us (5%)
  local copies, waits for them, and re-layouts  69 us (4%)
  starting transfers between devices  67 us (4%)
  other arithmetic  42.8 us (3%)
  between operations  19 us (1%)
    reduce_scatter x8, waiting for transfers between devices, shards(): lax.psum_scatter(jnp.einsum('th,td->hd', hidden_act, grad_result, preferr...  275 us
    reduce_scatter x8, waiting for transfers between devices, shards(): lax.psum_scatter(jnp.einsum('td,th->dh', normed_two, grad_pre, preferred_...  177 us
    all_gather x8, waiting for transfers between devices, output_of(): lax.all_gather(rows_out, 'dp', axis=0, tiled=True)  148 us
    psum x1, waiting for transfers between devices, shards(): lax.psum(shares[2].astype(jnp.bfloat16), 'seq').astype(jnp.float32)  145 us
    reduce_scatter x2, waiting for transfers between devices, shards(): lax.psum_scatter(packed_grad.astype(jnp.bfloat16), 'dp', scatter_dimensio...  83.4 us
    unnamed x43, waiting for transfers between devices  81.8 us
    dot_general x8, matrix products, hidden_of(): jnp.dot(normed_rows, lax.all_gather(rows_in, 'dp', axis=0, tiled=True), p...  76.2 us
    reduce_scatter x2, waiting for transfers between devices, shards(): lax.psum_scatter(out_grad.astype(jnp.bfloat16), 'dp', scatter_dimension=0...  72.3 us
  transfers between devices with their start and end apart: 57, of which 40 were waited for; matrix products, arithmetic and copies ran while one was open for 18% of the time, Pallas kernels for 0%

commit v1 on v0

v1 whole, which is shorter than its diff:
```python
import jax
import jax.numpy as jnp
from jax import lax
from jax.sharding import PartitionSpec as P

HEAD = 64
EPS = 1e-06
NEG = -1e30
META = 16
F32 = jnp.float32
BF16 = jnp.bfloat16


def normalize(values):
    center = values - jnp.mean(values, -1, keepdims=True)
    inverse = lax.rsqrt(jnp.mean(center * center, -1, keepdims=True) + EPS)
    return center * inverse, inverse


def norm_back(grad_unit, unit, inverse):
    return inverse * (
        grad_unit
        - jnp.mean(grad_unit, -1, keepdims=True)
        - unit * jnp.mean(grad_unit * unit, -1, keepdims=True)
    )


def heads_of(values):
    return values.reshape(values.shape[0], values.shape[1] // HEAD, HEAD)


def mm(form, left, right):
    return jnp.einsum(form, left, right, preferred_element_type=F32)


def gelu_and_slope(values):
    cdf = 0.5 * (1.0 + lax.erf(values * 0.7071067811865476))
    pdf = jnp.exp(-0.5 * values * values) * 0.3989422804014327
    return values * cdf, cdf + values * pdf


class Plan:
    def __init__(self, mesh, images, length):
        self.dp = mesh.shape["dp"]
        self.seq = mesh.shape["seq"]
        self.images = images
        self.piece = length // self.seq
        self.share = self.seq // images
        self.rows = images * self.piece
        self.groups = [
            [block * self.share + part for part in range(self.share)]
            for block in range(self.dp // self.share)
        ]

    def hops(self, turn):
        pairs = []
        for dp in range(self.dp):
            for seq in range(self.seq):
                local = (seq % self.images + turn) % self.images
                to_dp = dp // self.share * self.share + seq // self.images
                to_seq = dp % self.share * self.images + local
                pairs.append((dp * self.seq + seq, to_dp * self.seq + to_seq))
        return pairs

    def to_images(self, pieces):
        seq = lax.axis_index("seq") % self.images
        got = []
        for turn in range(self.images):
            piece = lax.dynamic_index_in_dim(pieces, (seq + turn) % self.images, 0, False)
            got.append(lax.ppermute(piece, ("dp", "seq"), self.hops(turn)))
        got = jnp.stack(got)
        return jnp.stack(
            [
                lax.dynamic_index_in_dim(got, (seq - slot) % self.images, 0, False)
                for slot in range(self.images)
            ]
        )

    def to_pieces(self, slots):
        seq = lax.axis_index("seq") % self.images
        got = []
        for turn in range(self.images):
            slot = lax.dynamic_index_in_dim(slots, (seq - turn) % self.images, 0, False)
            back = [(to, source) for source, to in self.hops(turn)]
            got.append(lax.ppermute(slot, ("dp", "seq"), back))
        got = jnp.stack(got)
        return jnp.stack(
            [
                lax.dynamic_index_in_dim(got, (local - seq) % self.images, 0, False)
                for local in range(self.images)
            ]
        )


def attention_scores(queries, keys_all, length):
    scores = mm("qhd,khd->hqk", heads_of(queries), heads_of(keys_all)) * HEAD ** (-0.5)
    valid = jnp.arange(keys_all.shape[0]) < length
    return jnp.where(valid[None, None, :], scores, NEG)


def build(mesh):
    def shards(
        tokens,
        cotangent,
        routes,
        token_mask,
        ln1_gain,
        ln1_bias,
        qkv_weight,
        out_weight,
        ln2_gain,
        ln2_bias,
        router_weight,
        expert_in,
        expert_out,
    ):
        images, piece, width = tokens.shape
        levels, experts = expert_in.shape[:2]
        length_all = token_mask.shape[1]
        plan = Plan(mesh, images, length_all)
        rows = plan.rows
        slice_hid = expert_out.shape[2]
        wide = experts * slice_hid
        part = lax.axis_index("dp") % plan.share

        start = lax.axis_index("seq") * piece
        local_valid = lax.dynamic_slice_in_dim(token_mask, start, piece, 1)
        chosen_all = jnp.sum(
            (routes[..., None] == jnp.arange(experts, dtype=jnp.int32)).astype(F32), -2
        )
        chosen_rows = jnp.transpose(chosen_all, (1, 0, 3, 2)).reshape(images, levels * experts, piece)
        lengths = jnp.sum(token_mask, -1)
        meta = jnp.zeros((images, META, width), F32)
        meta = meta.at[:, : levels * experts, :piece].set(chosen_rows)
        meta = meta.at[:, levels * experts, 0].set((lengths // 4).astype(F32))
        meta = meta.at[:, levels * experts + 1, 0].set((lengths % 4).astype(F32))
        masked = cotangent * local_valid[..., None].astype(BF16)
        slots = plan.to_images(jnp.concatenate([tokens, meta.astype(BF16), masked], 1))
        state = slots[:, :piece].reshape(rows, width).astype(F32)
        grad = slots[:, piece + META :].reshape(rows, width).astype(F32)
        meta = slots[:, piece : piece + META].astype(F32)
        chosen_in = meta[:, : levels * experts, :piece]
        chosen_in = jnp.transpose(
            chosen_in.reshape(images, levels, experts, piece), (1, 0, 3, 2)
        ).reshape(levels, rows, experts)
        length = meta[0, levels * experts, 0] * 4.0 + meta[0, levels * experts + 1, 0]
        length = length.astype(jnp.int32)

        vectors = jnp.stack([ln1_gain, ln1_bias, ln2_gain, ln2_bias], -1)
        dense = lax.all_gather(
            jnp.concatenate([qkv_weight, out_weight, vectors, router_weight], -1),
            "dp",
            axis=1,
            tiled=True,
        )
        proj_packed_all = dense[..., : 3 * width]
        proj_out_all = dense[..., 3 * width : 4 * width]
        vectors = jnp.swapaxes(dense[..., 4 * width : 4 * width + 4], 1, 2)
        router_all = dense[..., 4 * width + 4 :]
        up_all = lax.all_to_all(expert_in, "dp", split_axis=3, concat_axis=2, tiled=True)
        up_all = jnp.swapaxes(up_all, 1, 2).reshape(levels, width, wide)
        down_all = expert_out.reshape(levels, wide, width)

        saved = []
        for level in range(levels):
            gain_one, bias_one, gain_two, bias_two = vectors[level]
            unit_one, inverse_one = normalize(state)
            normed = (unit_one * gain_one + bias_one).astype(BF16)
            packed = mm("ld,de->le", normed, proj_packed_all[level]).astype(BF16)
            keys_values = lax.all_gather(
                packed[:, width:], "dp", axis=0, tiled=True, axis_index_groups=plan.groups
            )
            queries = packed[:, :width]
            keys_all, values_all = keys_values[:, :width], keys_values[:, width:]
            scores = attention_scores(queries, keys_all, length)
            highest = jnp.max(scores, -1, keepdims=True)
            expo = jnp.exp(scores - highest)
            totals = jnp.sum(expo, -1, keepdims=True)
            log_total = highest + jnp.log(totals)
            weights = (expo / totals).astype(BF16)
            mixed = mm("hqk,khd->qhd", weights, heads_of(values_all)).reshape(rows, width).astype(BF16)
            middle = state + mm("ld,de->le", mixed, proj_out_all[level])
            unit_two, inverse_two = normalize(middle)
            normed_two = (unit_two * gain_two + bias_two).astype(BF16)
            logits = mm("ld,de->le", normed_two, router_all[level])
            gates = jax.nn.softmax(logits, -1)
            chosen = chosen_in[level]
            combine = gates * chosen
            all_two = lax.all_gather(normed_two, "dp", axis=0, tiled=True)
            all_combine = lax.all_gather(combine, "dp", axis=0, tiled=True)
            spread = jnp.repeat(all_combine, slice_hid, axis=1)
            act, slope = gelu_and_slope(mm("td,dh->th", all_two, up_all[level]))
            act, slope = act.astype(BF16), slope.astype(BF16)
            scaled = (act * spread).astype(BF16)
            update = lax.psum_scatter(
                mm("th,hd->td", scaled, down_all[level]).astype(BF16),
                "dp",
                scatter_dimension=0,
                tiled=True,
            )
            state = middle + update.astype(F32)
            saved.append(
                dict(
                    unit_one=unit_one,
                    inverse_one=inverse_one,
                    normed=normed,
                    queries=queries,
                    keys_all=keys_all,
                    values_all=values_all,
                    log_total=log_total,
                    mixed=mixed,
                    unit_two=unit_two,
                    inverse_two=inverse_two,
                    normed_two=normed_two,
                    gates=gates,
                    chosen=chosen,
                    spread=spread,
                    all_two=all_two,
                    act=act,
                    slope=slope,
                    scaled=scaled,
                )
            )
        output = plan.to_pieces(state.astype(BF16).reshape(images, piece, width))

        grads = [None] * levels
        for level in reversed(range(levels)):
            kept = saved[level]
            gain_one, bias_one, gain_two, bias_two = vectors[level]
            all_grad = lax.all_gather(grad.astype(BF16), "dp", axis=0, tiled=True)
            grad_act = mm("td,hd->th", all_grad, down_all[level])
            grad_combine = jnp.sum(
                (grad_act * kept["act"]).reshape(-1, experts, slice_hid), -1
            )
            grad_pre = (grad_act * kept["spread"] * kept["slope"]).astype(BF16)
            up_grad = mm("td,th->dh", kept["all_two"], grad_pre)
            down_grad = mm("th,td->hd", kept["scaled"], all_grad)
            back = lax.psum_scatter(
                mm("th,dh->td", grad_pre, up_all[level]).astype(BF16),
                "dp",
                scatter_dimension=0,
                tiled=True,
            ).astype(F32)
            grad_combine = lax.psum_scatter(grad_combine, "dp", scatter_dimension=0, tiled=True)
            gates = kept["gates"]
            grad_gates = grad_combine * kept["chosen"]
            grad_logits = gates * (grad_gates - jnp.sum(gates * grad_gates, -1, keepdims=True))
            router = router_all[level].astype(F32)
            back = back + jnp.dot(grad_logits, router.T, precision=lax.Precision.HIGHEST)
            router_grad = jnp.dot(
                kept["normed_two"].astype(F32).T, grad_logits, precision=lax.Precision.HIGHEST
            )
            unit_two = kept["unit_two"]
            gain_two_grad = jnp.sum(back * unit_two, 0)
            bias_two_grad = jnp.sum(back, 0)
            grad_middle = grad + norm_back(back * gain_two, unit_two, kept["inverse_two"])
            grad_branch = grad_middle.astype(BF16)
            out_grad = mm("ld,le->de", kept["mixed"], grad_branch)
            grad_mixed = mm("le,de->ld", grad_branch, proj_out_all[level]).astype(BF16)
            queries, keys_all, values_all = kept["queries"], kept["keys_all"], kept["values_all"]
            probs = jnp.exp(attention_scores(queries, keys_all, length) - kept["log_total"])
            grad_split = heads_of(grad_mixed)
            grad_v = mm("hqk,qhd->khd", probs.astype(BF16), grad_split)
            grad_probs = mm("qhd,khd->hqk", grad_split, heads_of(values_all))
            grad_scores = (
                probs * (grad_probs - jnp.sum(probs * grad_probs, -1, keepdims=True))
            ).astype(BF16)
            scale = HEAD ** (-0.5)
            grad_q = scale * mm("hqk,khd->qhd", grad_scores, heads_of(keys_all))
            grad_k = scale * mm("hqk,qhd->khd", grad_scores, heads_of(queries))
            grad_kv = jnp.concatenate(
                [grad_k.reshape(length_all, width), grad_v.reshape(length_all, width)], -1
            )
            grad_kv = lax.psum_scatter(
                grad_kv.astype(BF16),
                "dp",
                scatter_dimension=0,
                tiled=True,
                axis_index_groups=plan.groups,
            )
            grad_packed = jnp.concatenate([grad_q.reshape(rows, width).astype(BF16), grad_kv], -1)
            back_one = mm("le,de->ld", grad_packed, proj_packed_all[level])
            packed_grad = mm("ld,le->de", kept["normed"], grad_packed)
            unit_one = kept["unit_one"]
            gain_one_grad = jnp.sum(back_one * unit_one, 0)
            bias_one_grad = jnp.sum(back_one, 0)
            grad = grad_middle + norm_back(back_one * gain_one, unit_one, kept["inverse_one"])
            vector_grads = jnp.stack(
                [gain_one_grad, bias_one_grad, gain_two_grad, bias_two_grad], -1
            )
            dense_grad = jnp.concatenate([packed_grad, out_grad, vector_grads, router_grad], -1)
            dense_grad = lax.psum_scatter(
                dense_grad.astype(BF16), "dp", scatter_dimension=0, tiled=True
            )
            up_grad = jnp.swapaxes(up_grad.astype(BF16).reshape(width, experts, slice_hid), 0, 1)
            up_grad = lax.all_to_all(up_grad, "dp", split_axis=1, concat_axis=2, tiled=True)
            grads[level] = (
                lax.psum(dense_grad, "seq").astype(F32),
                lax.psum(up_grad, "seq").astype(F32),
                lax.psum(
                    down_grad.astype(BF16).reshape(experts, slice_hid, width), "seq"
                ).astype(F32),
            )
        token_grad = plan.to_pieces(grad.astype(BF16).reshape(images, piece, width)).astype(F32)
        dense_grad, up_grad, down_grad = (jnp.stack(items) for items in zip(*grads))
        vector_grads = dense_grad[..., 4 * width : 4 * width + 4]
        return (
            output,
            token_grad,
            vector_grads[..., 0],
            vector_grads[..., 1],
            dense_grad[..., : 3 * width],
            dense_grad[..., 3 * width : 4 * width],
            vector_grads[..., 2],
            vector_grads[..., 3],
            dense_grad[..., 4 * width + 4 :],
            up_grad,
            down_grad,
        )

    return shards


def solution(mesh):
    return jax.shard_map(
        build(mesh),
        mesh=mesh,
        in_specs=(
            P("dp", "seq", None),
            P("dp", "seq", None),
            P(None, "dp", "seq", None),
            P("dp", None),
            P(None, "dp"),
            P(None, "dp"),
            P(None, "dp", None),
            P(None, "dp", None),
            P(None, "dp"),
            P(None, "dp"),
            P(None, "dp", None),
            P(None, None, "dp", None),
            P(None, None, "dp", None),
        ),
        out_specs=(
            P("dp", "seq", None),
            P("dp", "seq", None),
            P(None, "dp"),
            P(None, "dp"),
            P(None, "dp", None),
            P(None, "dp", None),
            P(None, "dp"),
            P(None, "dp"),
            P(None, "dp", None),
            P(None, None, "dp", None),
            P(None, None, "dp", None),
        ),
        check_vma=False,
    )
```

time: 1710 us -> 982 us (0.57)
  waiting for transfers between devices: 1170 us -> 614 us
  matrix products: 246 us -> 153 us
  blocking collectives: 86.5 us -> 17.8 us
  starting transfers between devices: 67 us -> 20 us
  local copies, waits for them, and re-layouts: 69 us -> 98.2 us
    reduce_scatter x20 -> x6, waiting for transfers between devices: 608 us -> 191 us  [the longest x2 88.2 us: shards(): lax.psum_scatter(mm('th,hd->td', scaled, down_all[level]).astype(BF16), '...]
    all_gather x18 -> x7, waiting for transfers between devices: 226 us -> 124 us  [the longest x2 54.6 us: shards(): all_grad = lax.all_gather(grad.astype(BF16), 'dp', axis=0, tiled=True)]
    dot_general x78 -> x42, matrix products: 246 us -> 153 us  [the longest x38 146 us: mm(): return jnp.einsum(form, left, right, preferred_element_type=F32)]
    all_to_all x16 -> x3, waiting for transfers between devices: 109 us -> 40.9 us  [the longest x1 30.4 us: shards(): lax.all_to_all(expert_in, 'dp', split_axis=3, concat_axis=2, tiled=True)]
    all_to_all x16 -> x3, starting transfers between devices: 64.8 us -> 11.1 us  [the longest x2 7.11 us: shards(): lax.all_to_all(up_grad, 'dp', split_axis=1, concat_axis=2, tiled=True)]
    unnamed x2 -> x0, blocking collectives: 28.6 us -> none
    psum x1, waiting for transfers between devices: 145 us -> 173 us  [shards(): lax.psum(dense_grad, 'seq').astype(F32)]
    all_gather x4 -> x2, blocking collectives: 45.1 us -> 17.8 us  [shards(): all_combine = lax.all_gather(combine, 'dp', axis=0, tiled=True)]
  transfers between devices with their start and end apart: 57 -> 27, of which waited for: 40 -> 20; matrix products, arithmetic and copies ran while one was open for 18% -> 15% of each run, Pallas kernels for 0% -> 0%
where the time goes in v1:
time: 982 us; the launch traced here: 973 us
  waiting for transfers between devices  614 us (63%)
  matrix products  153 us (16%)
  local copies, waits for them, and re-layouts  98.2 us (10%)
  other arithmetic  52.8 us (5%)
  starting transfers between devices  20 us (2%)
  blocking collectives  17.8 us (2%)
  between operations  17.5 us (2%)
    psum x1, waiting for transfers between devices, shards(): lax.psum(dense_grad, 'seq').astype(F32)  173 us
    dot_general x38, matrix products, mm(): return jnp.einsum(form, left, right, preferred_element_type=F32)  146 us
    reduce_scatter x2, waiting for transfers between devices, shards(): lax.psum_scatter(mm('th,hd->td', scaled, down_all[level]).astype(BF16), '...  88.2 us
    reduce_scatter x2, waiting for transfers between devices, shards(): lax.psum_scatter(mm('th,dh->td', grad_pre, up_all[level]).astype(BF16), '...  83.7 us
    unnamed x22, waiting for transfers between devices  73.8 us
    all_gather x2, waiting for transfers between devices, shards(): all_grad = lax.all_gather(grad.astype(BF16), 'dp', axis=0, tiled=True)  54.6 us
    unnamed x159, local copies, waits for them, and re-layouts  43.4 us
    all_to_all x1, waiting for transfers between devices, shards(): lax.all_to_all(expert_in, 'dp', split_axis=3, concat_axis=2, tiled=True)  30.4 us
  transfers between devices with their start and end apart: 27, of which 20 were waited for; matrix products, arithmetic and copies ran while one was open for 15% of the time, Pallas kernels for 0%

profile of v1, /device:TPU:0, one launch (start us, length us, event | category | flops | bytes accessed | tf_op | source)
XLA Modules:
  0.0 972.7 jit_solution(17425566871260132258)
XLA Ops:
  21.7 6.2 collective-permute-done.1
  28.7 25.0 %all-gather.10.cloned.1.call-done = bf16[2,512,2056]{2,1,0:T(8,128)(2,1)} async-done(((bf16[2,64,2056]{2,1,0:T(8,128)(2,1)}), bf16[2,512,2056]{2,1,0:T(8,128)(2,1)}) %all-gather.10.cloned.1.call-update) | async-done | bytes 4210704 | tf_op jit(solution)/shard_map/all_gather | solution.py:150
  60.7 7.4 all-gather.12.cloned.1.call-done
  77.6 7.0 copy.262
  84.6 7.6 reshape.577
  92.2 3.9 all-to-all-start
  99.4 30.4 %all-to-all-done = bf16[8,2,65536]{2,1,0:T(2,128)(2,1)S(1)} async-done(((bf16[8,2,65536]{2,1,0:T(2,128)(2,1)}), bf16[8,2,65536]{2,1,0:T(2,128)(2,1)S(1)}, u32[]{:S(2)}, u32[]{:S(2)}) %all-to-all-start) | async-done | bytes 2097184 | tf_op jit(solution)/shard_map/all_to_all | solution.py:160
  129.8 4.9 reshape.578
  134.7 5.6 copy.293
  145.1 8.4 all-gather
  153.6 8.8 fusion.10
  164.6 4.2 convolution_convert_fusion.3
  168.9 43.9 %reduce-scatter.19.cloned.1.call-done = bf16[320,512]{1,0:T(8,128)(2,1)} async-done(((bf16[2560,512]{1,0:T(8,128)(2,1)}), bf16[320,512]{1,0:T(8,128)(2,1)}) %reduce-scatter.19.cloned.1.call-update) | async-done | bytes 327696 | tf_op jit(solution)/shard_map/reduce_scatter | solution.py:195
  217.6 9.2 all-gather.16.cloned.1.call-done
  240.0 27.8 %all-gather.18.cloned.1.call-done = bf16[2560,512]{1,0:T(8,128)(2,1)} async-done(((bf16[320,512]{1,0:T(8,128)(2,1)}), bf16[2560,512]{1,0:T(8,128)(2,1)}) %all-gather.18.cloned.1.call-update) | async-done | bytes 2621456 | tf_op jit(solution)/shard_map/all_gather | solution.py:189
  267.8 8.8 fusion.90
  276.6 23.2 %all-gather.20.cloned.1.call-done = bf16[2560,512]{1,0:T(8,128)(2,1)} async-done(((bf16[320,512]{1,0:T(8,128)(2,1)}), bf16[2560,512]{1,0:T(8,128)(2,1)}) %all-gather.20.cloned.1.call-update) | async-done | bytes 2621456 | tf_op jit(solution)/shard_map/all_gather | solution.py:230
  299.8 11.7 %bitcast_reduce_fusion.1 = (f32[2560,4]{0,1:T(4,128)S(1)}, bf16[2560,1024]{0,1:T(8,128)(2,1)}, f32[2560,1024]{0,1:T(8,128)}) fusion(f32[2560,1024]{0,1:T(8,128)} %fusion.90, bf16[2560,512]{1,0:T(8,128)(2,1)} %all-gather.20.cloned.1.call-done, bf16[1024,512]{1,0:T(8,128)(2,1)S(1)} %bitcast.256), kind=kOutput, calls=%fused_computation.25 | convolution fusion | flops 2705315840 | bytes 29925376 | tf_op jit(solution)/shard_map/td,hd->th/dot_general | solution.py:33
  313.1 37.4 %reduce-scatter.31.cloned.1.call-done = f32[320,4]{1,0:T(8,128)} async-done(((f32[2560,4]{1,0:T(8,128)}), f32[320,4]{1,0:T(8,128)}) %reduce-scatter.31.cloned.1.call-update) | async-done | bytes 5136
  351.6 9.5 all-gather.1
  361.1 12.7 %fusion.15 = (bf16[2560,1024]{0,1:T(8,128)(2,1)S(1)}, bf16[2560,1024]{0,1:T(8,128)(2,1)}) fusion(f32[2560,1024]{0,1:T(8,128)} %get-tuple-element.216, f32[2560,1024]{0,1:T(8,128)} %fusion.90, f32[2560,4]{0,1:T(4,128)S(1)} %reshape.556, bf16[2560,1024]{0,1:T(8,128)(2,1)} %get-tuple-element.166), kind=kLoop, calls=%fused_computation.23 | loop fusion | flops 41943040 | bytes 36741120 | tf_op jit(solution)/shard_map/convert_element_type | solution.py:235
  376.2 4.2 convolution_convert_fusion.1
  380.5 6.8 convolution_convert_fusion.2
  387.4 36.9 %reduce-scatter.23.cloned.1.call-done = bf16[320,512]{1,0:T(8,128)(2,1)} async-done(((bf16[2560,512]{1,0:T(8,128)(2,1)}), bf16[320,512]{1,0:T(8,128)(2,1)}) %reduce-scatter.23.cloned.1.call-update) | async-done | bytes 327696 | tf_op jit(solution)/shard_map/reduce_scatter | solution.py:238
  427.4 44.3 %reduce-scatter.21.cloned.1.call-done = bf16[320,512]{1,0:T(8,128)(2,1)} async-done(((bf16[2560,512]{1,0:T(8,128)(2,1)}), bf16[320,512]{1,0:T(8,128)(2,1)}) %reduce-scatter.21.cloned.1.call-update) | async-done | bytes 327696 | tf_op jit(solution)/shard_map/reduce_scatter | solution.py:195
  478.2 4.2 fusion.32
  495.9 5.8 reduce-scatter.33.cloned.1.call-done
  503.1 3.6 multiply_reduce_fusion.3
  508.0 31.4 %all-gather.22.cloned.1.call-done = bf16[2560,512]{1,0:T(8,128)(2,1)} async-done(((bf16[320,512]{1,0:T(8,128)(2,1)}), bf16[2560,512]{1,0:T(8,128)(2,1)}) %all-gather.22.cloned.1.call-update) | async-done | bytes 2621456 | tf_op jit(solution)/shard_map/all_gather | solution.py:230
  539.4 10.0 %fusion.12 = (bf16[2560,1024]{0,1:T(8,128)(2,1)}, f32[2560,1024]{0,1:T(8,128)S(1)}) fusion(f32[2560,1024]{0,1:T(8,128)} %get-tuple-element.211, f32[2560,4]{0,1:T(4,128)S(1)} %reshape.554, bf16[2560,512]{1,0:T(8,128)(2,1)} %all-gather.22.cloned.1.call-done, bf16[1024,512]{1,0:T(8,128)(2,1)S(1)} %bitcast.251), kind=kOutput, calls=%fused_computation.20 | convolution fusion | flops 2718433280 | bytes 29925376 | tf_op jit(solution)/shard_map/td,hd->th/dot_general | solution.py:33
  549.4 4.3 bitcast_reduce_fusion
  555.3 6.8 convolution_convert_fusion
  562.4 30.3 %reduce-scatter.35.cloned.1.call-done = f32[320,4]{1,0:T(8,128)} async-done(((f32[2560,4]{1,0:T(8,128)}), f32[320,4]{1,0:T(8,128)}) %reduce-scatter.35.cloned.1.call-update) | async-done | bytes 5136
  593.7 46.8 %reduce-scatter.25.cloned.1.call-done = bf16[320,512]{1,0:T(8,128)(2,1)} async-done(((bf16[2560,512]{1,0:T(8,128)(2,1)}), bf16[320,512]{1,0:T(8,128)(2,1)}) %reduce-scatter.25.cloned.1.call-update) | async-done | bytes 327696 | tf_op jit(solution)/shard_map/reduce_scatter | solution.py:238
  648.7 4.2 fusion.35
  666.0 3.8 convolution_convert_fusion.4
  669.7 4.9 concatenate.43
  685.0 3.7 multiply_reduce_fusion.5
  691.5 3.9 concatenate.42
  695.4 6.5 convolution_convert_fusion.10
  707.0 6.2 convolution_convert_fusion.11
  714.9 10.5 %all-to-all-done.2 = bf16[4,512,256]{2,0,1:T(4,128)(2,1)S(1)} async-done(((bf16[4,512,256]{2,0,1:T(4,128)(2,1)}), bf16[4,512,256]{2,0,1:T(4,128)(2,1)S(1)}, u32[]{:S(2)}, u32[]{:S(2)}) %all-to-all-start.2) | async-done | bytes 1048608 | tf_op jit(solution)/shard_map/all_to_all | solution.py:296
  725.3 3.6 all-to-all-start.1
  729.2 7.3 convolution_convert_fusion.8
  740.5 7.1 convolution_convert_fusion.9
  749.6 18.8 %reduce-scatter.27.cloned.1.call-done = bf16[64,2056]{1,0:T(8,128)(2,1)} async-done(((bf16[512,2056]{1,0:T(8,128)(2,1)}), bf16[64,2056]{1,0:T(8,128)(2,1)}) %reduce-scatter.27.cloned.1.call-update) | async-done | bytes 263184 | tf_op jit(solution)/shard_map/reduce_scatter | solution.py:292
  774.3 4.1 collective-permute-done.5
  780.3 173.0 %all-reduce.4.cloned.1.call-done = (bf16[1,64,2056]{2,1,0:T(8,128)(2,1)}, bf16[1,64,2056]{2,1,0:T(8,128)(2,1)}, bf16[1,4,64,2048]{3,2,1,0:T(8,128)(2,1)}, bf16[1...) async-done(((bf16[1,64,2056]{2,1,0:T(8,128)(2,1)}, bf16[1,64,2056]{2,1,0:T(8,128)(2,1)}, ...) | async-done | bytes 4720656 | tf_op jit(solution)/shard_map/psum | solution.py:298
  (357 shorter events, 158.7 us)
Async XLA Ops:
  7.2 46.5 %all-gather.10.cloned.1.call-start = ((), (), s32[]{:S(2)}) async-start(), calls=%async_computation.13 | async-start | bytes 5013504 | tf_op jit(solution)/shard_map/all_gather | solution.py:150
  13.0 55.1 %all-gather.12.cloned.1.call-start = ((), (), s32[]{:S(2)}) async-start(), calls=%async_computation.14 | async-start | bytes 1966080 | tf_op jit(solution)/shard_map/all_gather | solution.py:170
  17.9 10.0 %collective-permute-start.1 = (bf16[336,512]{1,0:T(8,128)(2,1)S(1)}, bf16[336,512]{1,0:T(8,128)(2,1)S(1)}, u32[]{:S(2)}, u32[]{:S(2)}) collective-permute-start(bf16[336,512]{1,0:T(8,128)(2,1)S(1)} %get-tuple-element.185), channel_id=1, source_target_pairs={{0,1},{1,0},{2,5},{3,4},{4,3},{5,2},{6,7},{7,6},{8,9},{9,8},{10,13... | collective-permute-start | bytes 1032200 | tf_op jit(solution)/shard_map/ppermute | solution.py:70
  21.0 6.9 collective-permute-start
  28.2 32.6 %copy-start.20 = (bf16[1,336,512]{2,1,0:T(8,128)(2,1)}, bf16[1,336,512]{2,1,0:T(8,128)(2,1)S(1)}, u32[]{:S(2)}) copy-start(bf16[1,336,512]{2,1,0:T(8,128)(2,1)S(1)} %get-tuple-element.184) | copy-start | bytes 1032196
  28.3 46.4 %copy-start.16 = (bf16[2,160,512]{2,1,0:T(8,128)(2,1)}, bf16[2,160,512]{2,1,0:T(8,128)(2,1)S(1)}, u32[]{:S(2)}) copy-start(bf16[2,160,512]{2,1,0:T(8,128)(2,1)S(1)} %get-tuple-element.174) | copy-start | bytes 983044
  28.3 41.1 %copy-start.52 = (f32[2,160]{1,0:T(2,128)}, f32[2,160]{1,0:T(2,128)S(1)}, u32[]{:S(2)}) copy-start(f32[2,160]{1,0:T(2,128)S(1)} %broadcast_multiply_fusion.12) | copy-start | bytes 3844
  28.7 29.9 %copy-start.56 = (f32[2,160]{1,0:T(2,128)}, f32[2,160]{1,0:T(2,128)S(1)}, u32[]{:S(2)}) copy-start(f32[2,160]{1,0:T(2,128)S(1)} %add_rsqrt_fusion.3) | copy-start | bytes 3844
  55.3 14.2 %copy-start.58 = (f32[512]{0:T(512)}, f32[512]{0:T(512)S(1)}, u32[]{:S(2)}) copy-start(f32[512]{0:T(512)S(1)} %get-tuple-element.150) | copy-start | bytes 6148
  55.3 158.9 %copy-start.60 = (f32[512]{0:T(512)}, f32[512]{0:T(512)S(1)}, u32[]{:S(2)}) copy-start(f32[512]{0:T(512)S(1)} %get-tuple-element.146) | copy-start | bytes 6148
  58.6 95.0 %all-gather.14.cloned.1.call-start = ((), (), s32[]{:S(2)}) async-start(), calls=%async_computation.15 | async-start | bytes 2949120 | tf_op jit(solution)/shard_map/all_gather | solution.py:189
  74.7 17.4 %copy-start.43 = (bf16[8,64,320]{2,1,0:T(8,128)(2,1)}, bf16[8,64,320]{2,1,0:T(8,128)(2,1)S(1)}, u32[]{:S(2)}) copy-start(bf16[8,64,320]{2,1,0:T(8,128)(2,1)S(1)} %fusion.41) | copy-start | bytes 983044
  76.4 136.4 %copy-start.6 = (f32[320,512]{1,0:T(8,128)}, f32[320,512]{1,0:T(8,128)S(1)}, u32[]{:S(2)}) copy-start(f32[320,512]{1,0:T(8,128)S(1)} %get-tuple-element.208) | copy-start | bytes 1966084
  92.2 37.6 %all-to-all-start = ((bf16[8,2,65536]{2,1,0:T(2,128)(2,1)}), bf16[8,2,65536]{2,1,0:T(2,128)(2,1)S(1)}, u32[]{:S(2)}, u32[]{:S(2)}) async-start(bf16[8,2,65536]{2,1,0:T(2,128)(2,1)} %reshape.577), calls=%async_computation | async-start | bytes 4194304 | tf_op jit(solution)/shard_map/all_to_all | solution.py:160
  96.1 116.7 %reduce-scatter.19.cloned.1.call-start = ((), (), s32[]{:S(2)}) async-start(), calls=%async_computation.16 | async-start | bytes 2949120 | tf_op jit(solution)/shard_map/reduce_scatter | solution.py:195
  143.3 19.0 %copy-start.25 = (bf16[1,512,4,256]{1,3,2,0:T(8,128)(2,1)}, bf16[1,512,4,256]{1,3,2,0:T(8,128)(2,1)S(1)}, u32[]{:S(2)}) copy-start(bf16[1,512,4,256]{1,3,2,0:T(8,128)(2,1)S(1)} %copy.265) | copy-start | bytes 3145732
  153.6 11.1 %copy-start.27 = (bf16[1,4,256,512]{3,2,1,0:T(8,128)(2,1)S(1)}, bf16[1,4,256,512]{3,2,1,0:T(8,128)(2,1)}, u32[]{:S(2)}) copy-start(bf16[1,4,256,512]{3,2,1,0:T(8,128)(2,1)} %get-tuple-element.178) | copy-start | bytes 3145732
  168.9 58.0 %all-gather.16.cloned.1.call-start = ((), (), s32[]{:S(2)}) async-start(), calls=%async_computation.17 | async-start | bytes 1966080 | tf_op jit(solution)/shard_map/all_gather | solution.py:170
  213.9 19.6 %copy-start.8 = (f32[320,512]{1,0:T(8,128)}, f32[320,512]{1,0:T(8,128)S(1)}, u32[]{:S(2)}) copy-start(f32[320,512]{1,0:T(8,128)S(1)} %get-tuple-element.168) | copy-start | bytes 1966084
  217.3 50.5 %all-gather.18.cloned.1.call-start = ((), (), s32[]{:S(2)}) async-start(), calls=%async_computation.18 | async-start | bytes 2949120 | tf_op jit(solution)/shard_map/all_gather | solution.py:189
  217.6 12.5 %copy-start.33 = (bf16[320,512]{0,1:T(8,128)(2,1)}, bf16[320,512]{0,1:T(8,128)(2,1)S(1)}, u32[]{:S(2)}) copy-start(bf16[320,512]{0,1:T(8,128)(2,1)S(1)} %copy.269) | copy-start | bytes 983044
  236.4 63.5 %all-gather.20.cloned.1.call-start = ((), (), s32[]{:S(2)}) async-start(), calls=%async_computation.20 | async-start | bytes 2949120 | tf_op jit(solution)/shard_map/all_gather | solution.py:230
  237.2 113.3 %reduce-scatter.31.cloned.1.call-start = ((), (), s32[]{:S(2)}) async-start(), calls=%async_computation.26 | async-start | bytes 1474560
  267.8 32.0 %copy-start.30 = (bf16[1,4,256,512]{3,2,1,0:T(8,128)(2,1)S(1)}, bf16[1,4,256,512]{3,2,1,0:T(8,128)(2,1)}, u32[]{:S(2)}) copy-start(bf16[1,4,256,512]{3,2,1,0:T(8,128)(2,1)} %get-tuple-element.177) | copy-start | bytes 3145732
  313.0 111.3 %reduce-scatter.23.cloned.1.call-start = ((), (), s32[]{:S(2)}) async-start(), calls=%async_computation.21 | async-start | bytes 2949120 | tf_op jit(solution)/shard_map/reduce_scatter | solution.py:238
  361.1 15.1 %copy-start.45 = (bf16[1,512,4,256]{1,3,2,0:T(8,128)(2,1)S(1)}, bf16[1,512,4,256]{1,3,2,0:T(8,128)(2,1)}, u32[]{:S(2)}) copy-start(bf16[1,512,4,256]{1,3,2,0:T(8,128)(2,1)} %copy.271) | copy-start | bytes 3145732
  380.5 91.3 %reduce-scatter.21.cloned.1.call-start = ((), (), s32[]{:S(2)}) async-start(), calls=%async_computation.19 | async-start | bytes 2949120 | tf_op jit(solution)/shard_map/reduce_scatter | solution.py:195
  380.5 91.2 %copy-start.35 = (bf16[2,160,512]{2,1,0:T(8,128)(2,1)S(1)}, bf16[2,160,512]{2,1,0:T(8,128)(2,1)}, u32[]{:S(2)}) copy-start(bf16[2,160,512]{2,1,0:T(8,128)(2,1)} %pad_maximum_fusion.9) | copy-start | bytes 983044
  387.3 114.3 %reduce-scatter.33.cloned.1.call-start = ((), (), s32[]{:S(2)}) async-start(), calls=%async_computation.27 | async-start | bytes 1966080
  492.7 46.7 %all-gather.22.cloned.1.call-start = ((), (), s32[]{:S(2)}) async-start(), calls=%async_computation.22 | async-start | bytes 2949120 | tf_op jit(solution)/shard_map/all_gather | solution.py:230
  495.9 10.8 %copy-start.12 = (f32[320,512]{1,0:T(8,128)S(1)}, f32[320,512]{1,0:T(8,128)}, u32[]{:S(2)}) copy-start(f32[320,512]{1,0:T(8,128)} %copy-done.11) | copy-start | bytes 1966084
  503.1 36.3 %copy-start.28 = (bf16[1,4,256,512]{3,2,1,0:T(8,128)(2,1)S(1)}, bf16[1,4,256,512]{3,2,1,0:T(8,128)(2,1)}, u32[]{:S(2)}) copy-start(bf16[1,4,256,512]{3,2,1,0:T(8,128)(2,1)} %get-tuple-element.178) | copy-start | bytes 3145732
  507.9 84.7 %reduce-scatter.35.cloned.1.call-start = ((), (), s32[]{:S(2)}) async-start(), calls=%async_computation.28 | async-start | bytes 1474560
  555.2 85.3 %reduce-scatter.25.cloned.1.call-start = ((), (), s32[]{:S(2)}) async-start(), calls=%async_computation.23 | async-start | bytes 2949120 | tf_op jit(solution)/shard_map/reduce_scatter | solution.py:238
  555.2 85.2 %copy-start.7 = (f32[320,512]{1,0:T(8,128)S(1)}, f32[320,512]{1,0:T(8,128)}, u32[]{:S(2)}) copy-start(f32[320,512]{1,0:T(8,128)} %copy-done.6) | copy-start | bytes 1966084
  562.1 121.4 %reduce-scatter.37.cloned.1.call-start = ((), (), s32[]{:S(2)}) async-start(), calls=%async_computation.29 | async-start | bytes 1966080
  661.0 88.5 %reduce-scatter.29.cloned.1.call-start = ((), (), s32[]{:S(2)}) async-start(), calls=%async_computation.25 | async-start | bytes 2506752 | tf_op jit(solution)/shard_map/reduce_scatter | solution.py:292
  665.9 11.4 %copy-start.66 = (bf16[512]{0:T(512)(128)(2,1)S(1)}, bf16[512]{0:T(512)(128)(2,1)}, u32[]{:S(2)}) copy-start(bf16[512]{0:T(512)(128)(2,1)} %get-tuple-element.136) | copy-start | bytes 3076
  674.6 93.7 %reduce-scatter.27.cloned.1.call-start = ((), (), s32[]{:S(2)}) async-start(), calls=%async_computation.24 | async-start | bytes 2506752 | tf_op jit(solution)/shard_map/reduce_scatter | solution.py:292
  703.5 21.8 %all-to-all-start.2 = ((bf16[4,512,256]{2,0,1:T(4,128)(2,1)}), bf16[4,512,256]{2,0,1:T(4,128)(2,1)S(1)}, u32[]{:S(2)}, u32[]{:S(2)}) async-start(bf16[4,512,256]{2,0,1:T(4,128)(2,1)} %bitcast.83), calls=%async_computation.8 | async-start | bytes 2097152 | tf_op jit(solution)/shard_map/all_to_all | solution.py:296
  725.3 22.3 %all-to-all-start.1 = ((bf16[4,512,256]{2,0,1:T(4,128)(2,1)}), bf16[4,512,256]{2,0,1:T(4,128)(2,1)S(1)}, u32[]{:S(2)}, u32[]{:S(2)}) async-start(bf16[4,512,256]{2,0,1:T(4,128)(2,1)} %bitcast.80), calls=%async_computation.7 | async-start | bytes 2097152 | tf_op jit(solution)/shard_map/all_to_all | solution.py:296
  728.9 224.4 %all-reduce.4.cloned.1.call-start = ((), (), s32[]{:S(2)}) async-start(), calls=%async_computation.30 | async-start | bytes 9502720 | tf_op jit(solution)/shard_map/psum | solution.py:298
  747.6 20.8 %copy-start.44 = (bf16[320,512]{1,0:T(8,128)(2,1)S(1)}, bf16[320,512]{1,0:T(8,128)(2,1)}, u32[]{:S(2)}) copy-start(bf16[320,512]{1,0:T(8,128)(2,1)} %get-tuple-element.188) | copy-start | bytes 983044
  747.6 23.0 %copy-start.15 = (f32[320,512]{1,0:T(8,128)S(1)}, f32[320,512]{1,0:T(8,128)}, u32[]{:S(2)}) copy-start(f32[320,512]{1,0:T(8,128)} %copy-done.14) | copy-start | bytes 1966084
  768.4 5.9 collective-permute-start.3
  770.0 4.4 collective-permute-start.2
  772.1 6.3 collective-permute-start.5
  772.7 5.7 collective-permute-start.4
  (51 other events, 273.9 us)
Sparse Core Ops, SparseCore 0:
  13.1 40.5 all-gather.9
  58.7 9.4 all-gather.11
  77.7 43.9 all-gather.13
  169.0 43.7 reduce-scatter.18
  217.4 9.3 all-gather.15
  236.5 31.2 all-gather.17
  269.7 30.1 all-gather.19
  313.1 37.3 reduce-scatter.30
  380.6 43.6 reduce-scatter.22
  428.0 43.6 reduce-scatter.20
  492.8 8.7 reduce-scatter.32
  508.1 31.2 all-gather.21
  555.3 37.2 reduce-scatter.34
  596.8 43.6 reduce-scatter.24
  661.1 8.7 reduce-scatter.36
  674.8 47.6 reduce-scatter.28
  726.2 42.1 reduce-scatter.26
  771.0 182.2 all-reduce.3

commit v2 on v1

--- a/solution.py
+++ b/solution.py
@@ -1,6 +1,8 @@
 import jax
 import jax.numpy as jnp
 from jax import lax
+from jax.experimental import pallas as pl
+from jax.experimental.pallas import tpu as pltpu
 from jax.sharding import PartitionSpec as P
 
 HEAD = 64
@@ -33,10 +35,345 @@
     return jnp.einsum(form, left, right, preferred_element_type=F32)
 
 
-def gelu_and_slope(values):
-    cdf = 0.5 * (1.0 + lax.erf(values * 0.7071067811865476))
-    pdf = jnp.exp(-0.5 * values * values) * 0.3989422804014327
-    return values * cdf, cdf + values * pdf
+MESH = pl.DeviceIdType.MESH
+VMEM_LIMIT = 60 * 1024 * 1024
+
+
+def in_vmem():
+    return pl.BlockSpec(memory_space=pltpu.VMEM)
+
+
+def in_any():
+    return pl.BlockSpec(memory_space=pl.ANY)
+
+
+def greet(peers):
+    barrier = pltpu.get_barrier_semaphore()
+    for peer in peers:
+        pl.semaphore_signal(barrier, inc=1, device_id=peer, device_id_type=MESH)
+    pl.semaphore_wait(barrier, len(peers))
+
+
+def remote(src, dst, send, recv, peer):
+    return pltpu.make_async_remote_copy(
+        src_ref=src, dst_ref=dst, send_sem=send, recv_sem=recv, device_id=peer, device_id_type=MESH
+    )
+
+
+def split_rows(rows8):
+    high = rows8.astype(BF16).astype(F32)
+    return jnp.concatenate([high, rows8 - high], 0).astype(BF16)
+
+
+def join_rows(rows16):
+    wide = rows16.astype(F32)
+    return wide[:8] + wide[8:]
+
+
+def gelu_parts(u):
+    x = jnp.abs(u) * 0.7071067811865476
+    bell = jnp.exp(-x * x)
+    t = 1.0 / (1.0 + 0.3275911 * x)
+    poly = t * (
+        0.254829592 + t * (-0.284496736 + t * (1.421413741 + t * (-1.453152027 + t * 1.061405429)))
+    )
+    half = 0.5 * poly * bell
+    cdf = jnp.where(u >= 0, 1.0 - half, half)
+    return u * cdf, cdf + u * bell * 0.3989422804014327
+
+
+def dot(left, right, dims=((1,), (0,))):
+    return lax.dot_general(left, right, (dims, ((), ())), preferred_element_type=F32)
+
+
+class Group:
+    def __init__(self, size):
+        self.size = size
+        self.pairs = size // 2
+
+    def peers(self):
+        me = lax.axis_index("dp")
+        return [{"dp": me ^ 1}] + [{"dp": me ^ (2 * pair)} for pair in range(1, self.pairs)]
+
+    def scratch(self, rows, tail, width):
+        full = rows + tail
+        return [
+            pltpu.VMEM((self.pairs, rows, width), F32),
+            pltpu.VMEM((self.pairs, 16, width), F32),
+            pltpu.VMEM((self.pairs, full, width), BF16),
+            pltpu.VMEM((self.pairs, full, width), BF16),
+            pltpu.VMEM((self.pairs, full, width), BF16),
+            pltpu.VMEM((self.pairs, full, width), BF16),
+            pltpu.SemaphoreType.DMA((self.size,)),
+            pltpu.SemaphoreType.DMA((self.size,)),
+            pltpu.SemaphoreType.DMA((self.size,)),
+            pltpu.SemaphoreType.DMA((self.pairs,)),
+            pltpu.SemaphoreType.DMA((self.pairs,)),
+            pltpu.SemaphoreType.DMA((self.pairs,)),
+            pltpu.SemaphoreType.DMA((self.pairs,)),
+        ]
+
+    def run(self, slots, scratch, rows, tail, compute):
+        own, own_tail, give, take, pay, due, send, recv, hand, g_send, g_recv, p_send, p_recv = scratch
+        me = lax.axis_index("dp")
+        next_core = {"dp": me ^ 1}
+
+        def block(slot, peer):
+            return remote(slots.at[0], slots.at[slot], send.at[slot], recv.at[slot], peer)
+
+        def handed(slot):
+            return remote(slots.at[slot], slots.at[slot + 1], hand.at[slot], recv.at[slot + 1], next_core)
+
+        def given(pair):
+            return remote(give.at[pair], take.at[pair], g_send.at[pair], g_recv.at[pair], next_core)
+
+        def paid(pair):
+            owner = {"dp": me ^ (2 * pair)}
+            return remote(pay.at[pair], due.at[pair], p_send.at[pair], p_recv.at[pair], owner)
+
+        def settle(pair):
+            given(pair).wait_recv()
+            own[pair] += take[pair, :rows].astype(F32)
+            if tail:
+                own_tail[pair, :8] += join_rows(take[pair, rows:])
+
+            @pl.when(pair > 0)
+            def _():
+                pay[pair, :rows] = own[pair].astype(BF16)
+                if tail:
+                    pay[pair, rows:] = split_rows(own_tail[pair, :8])
+                paid(pair).start()
+
+        block(1, next_core).start()
+        for pair in range(1, self.pairs):
+            block(2 * pair, {"dp": me ^ (2 * pair)}).start()
+
+        def step(slot, carry):
+            pair = slot // 2
+            even = lax.rem(slot, 2) == 0
+
+            @pl.when(slot > 0)
+            def _():
+                block(slot, next_core).wait_recv()
+
+            @pl.when(even & (slot > 0))
+            def _():
+                handed(slot).start()
+
+            total, total_tail = compute(slot)
+
+            @pl.when(even)
+            def _():
+                own[pair] = total
+                if tail:
+                    own_tail[pair, :8] = total_tail
+
+            @pl.when(jnp.logical_not(even))
+            def _():
+                give[pair, :rows] = total.astype(BF16)
+                if tail:
+                    give[pair, rows:] = split_rows(total_tail)
+                given(pair).start()
+
+            @pl.when(even & (slot > 0))
+            def _():
+                settle(pair - 1)
+
+            return carry
+
+        lax.fori_loop(0, self.size, step, 0)
+        settle(self.pairs - 1)
+
+    def collect(self, scratch, slots, rows, tail):
+        own, own_tail, give, take, pay, due, send, recv, hand, g_send, g_recv, p_send, p_recv = scratch
+        me = lax.axis_index("dp")
+        next_core = {"dp": me ^ 1}
+        for pair in range(1, self.pairs):
+            remote(pay.at[pair], due.at[pair], p_send.at[pair], p_recv.at[pair], next_core).wait_recv()
+            own[0] += due[pair, :rows].astype(F32)
+            if tail:
+                own_tail[0, :8] += join_rows(due[pair, rows:])
+        for pair in range(self.pairs):
+            remote(give.at[pair], take.at[pair], g_send.at[pair], g_recv.at[pair], next_core).wait_send()
+            if pair:
+                remote(
+                    pay.at[pair], due.at[pair], p_send.at[pair], p_recv.at[pair], next_core
+                ).wait_send()
+                slot = 2 * pair
+                remote(
+                    slots.at[slot], slots.at[slot], send.at[slot], recv.at[slot], next_core
+                ).wait_send()
+                remote(
+                    slots.at[slot], slots.at[slot], hand.at[slot], recv.at[slot], next_core
+                ).wait_send()
+        remote(slots.at[1], slots.at[1], send.at[1], recv.at[1], next_core).wait_send()
+
+
+def experts_forward(message, middle, up, down, size, experts):
+    rows, width = middle.shape
+    wide = up.shape[1]
+    hid = wide // experts
+    group = Group(size)
+
+    def kernel(msg_ref, mid_ref, up_ref, down_ref, out_ref, all_ref, act_ref, slope_ref, *scratch):
+        slots, act, slope, scaled, save_sem = scratch[:5]
+        scratch = scratch[5:]
+        greet(group.peers())
+        slots[0] = msg_ref[...]
+
+        def saves(slot):
+            return (
+                pltpu.make_async_copy(slots.at[slot], all_ref.at[slot], save_sem.at[slot, 0]),
+                pltpu.make_async_copy(act.at[slot], act_ref.at[slot], save_sem.at[slot, 1]),
+                pltpu.make_async_copy(slope.at[slot], slope_ref.at[slot], save_sem.at[slot, 2]),
+            )
+
+        def compute(slot):
+            gates = jnp.transpose(join_rows(slots[slot, rows:]))[:rows]
+            for expert in range(experts):
+                cols = slice(expert * hid, (expert + 1) * hid)
+                value, grade = gelu_parts(dot(slots[slot, :rows], up_ref[:, cols]))
+                value = value.astype(BF16)
+                act[slot, :, cols] = value
+                slope[slot, :, cols] = grade.astype(BF16)
+                scaled[:, cols] = (value.astype(F32) * gates[:, expert : expert + 1]).astype(BF16)
+            for save in saves(slot):
+                save.start()
+            return dot(scaled[...], down_ref[...]), None
+
+        group.run(slots, scratch, rows, 0, compute)
+        group.collect(scratch, slots, rows, 0)
+        out_ref[...] = mid_ref[...] + scratch[0][0]
+        for slot in range(size):
+            for save in saves(slot):
+                save.wait()
+
+    return pl.pallas_call(
+        kernel,
+        out_shape=(
+            jax.ShapeDtypeStruct((rows, width), F32),
+            jax.ShapeDtypeStruct((size, rows + META, width), BF16),
+            jax.ShapeDtypeStruct((size, rows, wide), BF16),
+            jax.ShapeDtypeStruct((size, rows, wide), BF16),
+        ),
+        in_specs=[in_vmem()] * 4,
+        out_specs=(in_vmem(), in_any(), in_any(), in_any()),
+        scratch_shapes=[
+            pltpu.VMEM((size, rows + META, width), BF16),
+            pltpu.VMEM((size, rows, wide), BF16),
+            pltpu.VMEM((size, rows, wide), BF16),
+            pltpu.VMEM((rows, wide), BF16),
+            pltpu.SemaphoreType.DMA((size, 3)),
+        ]
+        + group.scratch(rows, 0, width),
+        compiler_params=pltpu.CompilerParams(
+            collective_id=1, has_side_effects=True, vmem_limit_bytes=VMEM_LIMIT
+        ),
+        name="experts_forward",
+    )(message, middle, up, down)
+
+
+def experts_backward(grad, blocks, act, slope, up, down, size, experts):
+    rows, width = grad.shape
+    wide = up.shape[1]
+    hid = wide // experts
+    group = Group(size)
+
+    def kernel(
+        grad_ref, blocks_ref, act_ref, slope_ref, up_ref, down_ref,
+        out_ref, tail_ref, up_out, down_out, *scratch,
+    ):
+        slots, blocks, act, slope, weighed, scaled, pre, load_sem = scratch[:8]
+        scratch = scratch[8:]
+
+        def loads(slot):
+            two = lax.rem(slot, 2)
+            return (
+                pltpu.make_async_copy(blocks_ref.at[slot], blocks.at[slot], load_sem.at[two, 0]),
+                pltpu.make_async_copy(act_ref.at[slot], act.at[two], load_sem.at[two, 1]),
+                pltpu.make_async_copy(slope_ref.at[slot], slope.at[two], load_sem.at[two, 2]),
+            )
+
+        for load in loads(0):
+            load.start()
+        greet(group.peers())
+        slots[0] = grad_ref[...]
+        lane = lax.broadcasted_iota(jnp.int32, (16, wide), 1) // hid
+        pick = (lane == lax.broadcasted_iota(jnp.int32, (16, wide), 0)).astype(F32).astype(BF16)
+
+        def compute(slot):
+            two = lax.rem(slot, 2)
+
+            @pl.when(slot + 1 < size)
+            def _():
+                for load in loads(slot + 1):
+                    load.start()
+
+            for load in loads(slot):
+                load.wait()
+            gates = jnp.transpose(join_rows(blocks[slot, rows:]))[:rows]
+            place = pl.ds(pl.multiple_of(slot * rows, 16), rows)
+            for expert in range(experts):
+                cols = slice(expert * hid, (expert + 1) * hid)
+                gate = gates[:, expert : expert + 1]
+                pull = dot(slots[slot], down_ref[cols, :], ((1,), (1,)))
+                value = act[two, :, cols].astype(F32)
+                weighed[:, cols] = (pull * value).astype(BF16)
+                scaled[place, cols] = (value * gate).astype(BF16)
+                pre[place, cols] = (pull * gate * slope[two, :, cols].astype(F32)).astype(BF16)
+            by_expert = dot(pick, weighed[...], ((1,), (1,)))[:8]
+            if rows < width:
+                by_expert = jnp.concatenate([by_expert, jnp.zeros((8, width - rows), F32)], 1)
+            return dot(pre[place, :], up_ref[...], ((1,), (1,))), by_expert
+
+        group.run(slots, scratch, rows, 16, compute)
+
+        for expert in range(experts):
+            cols = slice(expert * hid, (expert + 1) * hid)
+            up_sum = jnp.zeros((width, hid), F32)
+            down_sum = jnp.zeros((hid, width), F32)
+
+            def add(slot, sums):
+                place = pl.ds(pl.multiple_of(slot * rows, 16), rows)
+                return (
+                    sums[0] + dot(blocks[slot, :rows], pre[place, cols], ((0,), (0,))),
+                    sums[1] + dot(scaled[place, cols], slots[slot], ((0,), (0,))),
+                )
+
+            up_sum, down_sum = lax.fori_loop(0, size, add, (up_sum, down_sum))
+            up_out[:, cols] = up_sum.astype(BF16)
+            down_out[cols, :] = down_sum.astype(BF16)
+
+        group.collect(scratch, slots, rows, 16)
+        out_ref[...] = scratch[0][0]
+        tail_ref[...] = scratch[1][0, :8]
+
+    return pl.pallas_call(
+        kernel,
+        out_shape=(
+            jax.ShapeDtypeStruct((rows, width), F32),
+            jax.ShapeDtypeStruct((8, width), F32),
+            jax.ShapeDtypeStruct((width, wide), BF16),
+            jax.ShapeDtypeStruct((wide, width), BF16),
+        ),
+        in_specs=[in_vmem(), in_any(), in_any(), in_any(), in_vmem(), in_vmem()],
+        out_specs=(in_vmem(),) * 4,
+        scratch_shapes=[
+            pltpu.VMEM((size, rows, width), BF16),
+            pltpu.VMEM((size, rows + META, width), BF16),
+            pltpu.VMEM((2, rows, wide), BF16),
+            pltpu.VMEM((2, rows, wide), BF16),
+            pltpu.VMEM((rows, wide), BF16),
+            pltpu.VMEM((size * rows, wide), BF16),
+            pltpu.VMEM((size * rows, wide), BF16),
+            pltpu.SemaphoreType.DMA((2, 3)),
+        ]
+        + group.scratch(rows, 16, width),
+        compiler_params=pltpu.CompilerParams(
+            collective_id=2, has_side_effects=True, vmem_limit_bytes=VMEM_LIMIT
+        ),
+        name="experts_backward",
+    )(grad, blocks, act, slope, up, down)
 
 
 class Plan:
@@ -186,19 +523,11 @@
             gates = jax.nn.softmax(logits, -1)
             chosen = chosen_in[level]
             combine = gates * chosen
-            all_two = lax.all_gather(normed_two, "dp", axis=0, tiled=True)
-            all_combine = lax.all_gather(combine, "dp", axis=0, tiled=True)
-            spread = jnp.repeat(all_combine, slice_hid, axis=1)
-            act, slope = gelu_and_slope(mm("td,dh->th", all_two, up_all[level]))
-            act, slope = act.astype(BF16), slope.astype(BF16)
-            scaled = (act * spread).astype(BF16)
-            update = lax.psum_scatter(
-                mm("th,hd->td", scaled, down_all[level]).astype(BF16),
-                "dp",
-                scatter_dimension=0,
-                tiled=True,
-            )
-            state = middle + update.astype(F32)
+            gate_rows = jnp.zeros((8, width), F32).at[:experts, :rows].set(combine.T)
+            message = jnp.concatenate([normed_two, split_rows(gate_rows)], 0)
+            state, blocks, act, slope = experts_forward(
+                message, middle, up_all[level], down_all[level], plan.dp, experts
+            )
             saved.append(
                 dict(
                     unit_one=unit_one,
@@ -214,11 +543,9 @@
                     normed_two=normed_two,
                     gates=gates,
                     chosen=chosen,
-                    spread=spread,
-                    all_two=all_two,
+                    blocks=blocks,
                     act=act,
                     slope=slope,
-                    scaled=scaled,
                 )
             )
         output = plan.to_pieces(state.astype(BF16).reshape(images, piece, width))
@@ -227,21 +554,17 @@
         for level in reversed(range(levels)):
             kept = saved[level]
             gain_one, bias_one, gain_two, bias_two = vectors[level]
-            all_grad = lax.all_gather(grad.astype(BF16), "dp", axis=0, tiled=True)
-            grad_act = mm("td,hd->th", all_grad, down_all[level])
-            grad_combine = jnp.sum(
-                (grad_act * kept["act"]).reshape(-1, experts, slice_hid), -1
-            )
-            grad_pre = (grad_act * kept["spread"] * kept["slope"]).astype(BF16)
-            up_grad = mm("td,th->dh", kept["all_two"], grad_pre)
-            down_grad = mm("th,td->hd", kept["scaled"], all_grad)
-            back = lax.psum_scatter(
-                mm("th,dh->td", grad_pre, up_all[level]).astype(BF16),
-                "dp",
-                scatter_dimension=0,
-                tiled=True,
-            ).astype(F32)
-            grad_combine = lax.psum_scatter(grad_combine, "dp", scatter_dimension=0, tiled=True)
+            back, back_tail, up_grad, down_grad = experts_backward(
+                grad.astype(BF16),
+                kept["blocks"],
+                kept["act"],
+                kept["slope"],
+                up_all[level],
+                down_all[level],
+                plan.dp,
+                experts,
+            )
+            grad_combine = back_tail[:experts, :rows].T
             gates = kept["gates"]
             grad_gates = grad_combine * kept["chosen"]
             grad_logits = gates * (grad_gates - jnp.sum(gates * grad_gates, -1, keepdims=True))

time: 982 us -> 708 us (0.72)
  waiting for transfers between devices: 614 us -> 293 us
  Pallas kernels: 0 us -> 180 us
  matrix products: 153 us -> 60.8 us
  blocking collectives: 17.8 us -> 0 us
  other arithmetic: 52.8 us -> 39 us
    pallas_call x0 -> x4, Pallas kernels: none -> 180 us  [the longest x2 91.6 us: experts_backward(): pl.pallas_call(kernel, out_shape=(jax.ShapeDtypeStruct((rows, width), F32...]
    reduce_scatter x4 -> x0, waiting for transfers between devices: 172 us -> none  [the longest x2 88.2 us: shards(): lax.psum_scatter(mm('th,hd->td', scaled, down_all[level]).astype(BF16), '...]
    dot_general x38 -> x26, matrix products: 146 us -> 54.5 us  [mm(): return jnp.einsum(form, left, right, preferred_element_type=F32)]
    all_gather x4 -> x0, waiting for transfers between devices: 82.4 us -> none  [the longest x2 54.6 us: shards(): all_grad = lax.all_gather(grad.astype(BF16), 'dp', axis=0, tiled=True)]
    unnamed x22 -> x10, waiting for transfers between devices: 73.8 us -> 6.1 us
    all_to_all x1, waiting for transfers between devices: 30.4 us -> 0.01 us  [shards(): lax.all_to_all(expert_in, 'dp', split_axis=3, concat_axis=2, tiled=True)]
    reduce_scatter x2, waiting for transfers between devices: 18.8 us -> 41.4 us  [shards(): lax.psum_scatter(dense_grad.astype(BF16), 'dp', scatter_dimension=0, tile...]
    all_to_all x2, waiting for transfers between devices: 10.5 us -> 32.4 us  [shards(): lax.all_to_all(up_grad, 'dp', split_axis=1, concat_axis=2, tiled=True)]
  transfers between devices with their start and end apart: 27 -> 17, of which waited for: 20 -> 9; matrix products, arithmetic and copies ran while one was open for 15% -> 13% of each run, Pallas kernels for 0% -> 0%
where the time goes in v2:
time: 708 us; the launch traced here: 702 us
  waiting for transfers between devices  293 us (41%)
  Pallas kernels  180 us (25%)
  local copies, waits for them, and re-layouts  89.8 us (13%)
  matrix products  60.8 us (9%)
  other arithmetic  39 us (6%)
  starting transfers between devices  22.1 us (3%)
  between operations  17.6 us (2%)
    psum x1, waiting for transfers between devices, shards(): lax.psum(dense_grad, 'seq').astype(F32)  174 us
    pallas_call x2, Pallas kernels, experts_backward(): pl.pallas_call(kernel, out_shape=(jax.ShapeDtypeStruct((rows, width), F32...  91.6 us
    pallas_call x2, Pallas kernels, experts_forward(): pl.pallas_call(kernel, out_shape=(jax.ShapeDtypeStruct((rows, width), F32...  87.9 us
    dot_general x26, matrix products, mm(): return jnp.einsum(form, left, right, preferred_element_type=F32)  54.5 us
    reduce_scatter x2, waiting for transfers between devices, shards(): lax.psum_scatter(dense_grad.astype(BF16), 'dp', scatter_dimension=0, tile...  41.4 us
    unnamed x195, local copies, waits for them, and re-layouts  36.9 us
    all_to_all x2, waiting for transfers between devices, shards(): lax.all_to_all(up_grad, 'dp', split_axis=1, concat_axis=2, tiled=True)  32.4 us
    all_gather x1, waiting for transfers between devices, shards(): lax.all_gather(jnp.concatenate([qkv_weight, out_weight, vectors, router_w...  24.9 us
  transfers between devices with their start and end apart: 17, of which 9 were waited for; matrix products, arithmetic and copies ran while one was open for 13% of the time, Pallas kernels for 0%

profile of v2, /device:TPU:0, one launch (start us, length us, event | category | flops | bytes accessed | tf_op | source)
XLA Modules:
  0.0 701.5 jit_solution(3580695789797945149)
XLA Ops:
  11.3 1.9 concatenate.53
  18.0 3.1 collective-permute-start.1
  22.4 4.8 copy.209
  27.2 7.6 %reshape.608 = bf16[8,2,65536]{2,1,0:T(2,128)(2,1)} reshape(bf16[2048,2,4,64]{3,2,1,0:T(4,128)(2,1)} %bitcast.206) | data formatting | bytes 4194304
  34.8 6.0 all-to-all-start
  42.6 24.9 %all-gather.4.cloned.1.call-done = bf16[2,512,2056]{2,1,0:T(8,128)(2,1)} async-done(((bf16[2,64,2056]{2,1,0:T(8,128)(2,1)}), bf16[2,512,2056]{2,1,0:T(8,128)(2,1)}) %all-gather.4.cloned.1.call-update) | async-done | bytes 4210704 | tf_op jit(solution)/shard_map/all_gather | solution.py:487
  69.4 2.1 convolution_convert_fusion.3
  73.6 3.0 fusion.60
  78.6 5.0 reshape.609
  83.5 6.4 copy.210
  93.1 2.3 fusion.63
  101.9 1.8 fusion.25
  108.1 46.6 %experts_forward.2 = (f32[320,512]{1,0:T(8,128)}, bf16[8,336,512]{2,1,0:T(8,128)(2,1)}, bf16[8,320,1024]{2,1,0:T(8,128)(2,1)}, bf16[8,320,1024]{2,1,0:T(8,128)(2,1)}) custom-call(bf16[336,512]{1,0:T(8,128)(2,1)} %pad_maximum_fusion.9.msg_ref, f32[320,512]{1,0:T(8,128)} %copy-done.8, bf16[512,1024]{1,0:T(8,128)(2,1)} %bitcast.207, bf16[1024,512]{1,0:T(8,128)(2,1)} %bitcast.211), custom_call_target="tpu_custom_call" | custom-call | tf_op jit(solution)/shard_map/experts_forward/pallas_call | solution.py:251
  157.4 2.4 convolution_convert_fusion.2
  164.1 8.8 %all-gather.8.cloned.1.call-done = bf16[640,1024]{1,0:T(8,128)(2,1)} async-done(((bf16[320,1024]{1,0:T(8,128)(2,1)}), bf16[640,1024]{1,0:T(8,128)(2,1)}) %all-gather.8.cloned.1.call-update) | async-done | bytes 1310736 | tf_op jit(solution)/shard_map/all_gather | solution.py:507
  176.1 1.9 fusion.1
  185.0 41.3 %experts_forward.3 = (f32[320,512]{1,0:T(8,128)}, bf16[8,336,512]{2,1,0:T(8,128)(2,1)}, bf16[8,320,1024]{2,1,0:T(8,128)(2,1)}, bf16[8,320,1024]{2,1,0:T(8,128)(2,1)}) custom-call(bf16[336,512]{1,0:T(8,128)(2,1)} %pad_maximum_fusion.10.msg_ref, f32[320,512]{1,0:T(8,128)} %copy-done.6, bf16[512,1024]{1,0:T(8,128)(2,1)} %bitcast.209, bf16[1024,512]{1,0:T(8,128)(2,1)} %bitcast.213), custom_call_target="tpu_custom_call" | custom-call | tf_op jit(solution)/shard_map/experts_forward/pallas_call | solution.py:251
  226.4 45.7 %experts_backward.2 = (f32[320,512]{1,0:T(8,128)}, f32[8,512]{1,0:T(8,128)}, bf16[512,1024]{1,0:T(8,128)(2,1)}, bf16[1024,512]{1,0:T(8,128)(2,1)}) custom-call(bf16[320,512]{1,0:T(8,128)(2,1)} %bitcast.237, bf16[8,336,512]{2,1,0:T(8,128)(2,1)} %get-tuple-element.89.blocks_ref, bf16[8,320,1024]{2,1,0:T(8,128)(2,1)} %get-tuple-element.90.act_ref, ...), custom_call_target="tpu_custom_call" | custom-call | tf_op jit(solution)/shard_map/experts_backward/pallas_call | solution.py:351
  273.5 2.6 multiply_reduce_fusion.2
  278.9 4.2 fusion.16
  283.2 2.3 multiply_reduce_fusion.1
  290.9 2.7 copy.234
  293.7 2.9 fusion.22
  296.6 6.0 reduce-scatter.13.cloned.1.call-done
  304.1 3.0 multiply_reduce_fusion.3
  308.4 45.9 %experts_backward.3 = (f32[320,512]{1,0:T(8,128)}, f32[8,512]{1,0:T(8,128)}, bf16[512,1024]{1,0:T(8,128)(2,1)}, bf16[1024,512]{1,0:T(8,128)(2,1)}) custom-call(bf16[320,512]{1,0:T(8,128)(2,1)} %get-tuple-element.203.grad_ref, bf16[8,336,512]{2,1,0:T(8,128)(2,1)} %get-tuple-element.94.blocks_ref, bf16[8,320,1024]{2,1,0:T(8,128)(2,1)} %get-tuple-element.95.act_ref, ...), custom_call_target="tpu_custom_call" | custom-call | tf_op jit(solution)/shard_map/experts_backward/pallas_call | solution.py:351
  355.9 2.0 multiply_reduce_fusion.4
  360.3 2.1 convolution_convert_fusion.6
  363.6 4.2 fusion.19
  367.9 2.2 multiply_reduce_fusion
  377.5 3.4 convolution_convert_fusion
  380.8 4.4 concatenate.61
  389.0 2.4 convolution_convert_fusion.5
  391.4 2.9 fusion.23
  395.8 3.5 multiply_reduce_fusion.5
  402.2 3.9 concatenate.60
  406.1 2.7 reshape.576
  408.8 3.9 all-to-all-start.2
  414.3 18.1 %all-to-all-done.2 = bf16[4,512,256]{2,0,1:T(4,128)(2,1)S(1)} async-done(((bf16[4,512,256]{2,0,1:T(4,128)(2,1)}), bf16[4,512,256]{2,0,1:T(4,128)(2,1)S(1)}, u32[]{:S(2)}, u32[]{:S(2)}) %all-to-all-start.2) | async-done | bytes 1048608 | tf_op jit(solution)/shard_map/all_to_all | solution.py:619
  432.4 3.6 all-to-all-start.1
  437.6 2.3 stack.157
  439.9 14.3 %all-to-all-done.1 = bf16[4,512,256]{2,0,1:T(4,128)(2,1)S(1)} async-done(((bf16[4,512,256]{2,0,1:T(4,128)(2,1)}), bf16[4,512,256]{2,0,1:T(4,128)(2,1)S(1)}, u32[]{:S(2)}, u32[]{:S(2)}) %all-to-all-start.1) | async-done | bytes 1048608 | tf_op jit(solution)/shard_map/all_to_all | solution.py:619
  456.2 41.4 %reduce-scatter.9.cloned.1.call-done = bf16[64,2056]{1,0:T(8,128)(2,1)} async-done(((bf16[512,2056]{1,0:T(8,128)(2,1)}), bf16[64,2056]{1,0:T(8,128)(2,1)}) %reduce-scatter.9.cloned.1.call-update) | async-done | bytes 263184 | tf_op jit(solution)/shard_map/reduce_scatter | solution.py:615
  501.6 2.0 collective-permute-done.3
  503.6 3.2 collective-permute-done.5
  508.6 173.9 %all-reduce.6.cloned.1.call-done = (bf16[1,64,2056]{2,1,0:T(8,128)(2,1)}, bf16[1,64,2056]{2,1,0:T(8,128)(2,1)}, bf16[1,4,64,2048]{3,2,1,0:T(8,128)(2,1)}, bf16[1...) async-done(((bf16[1,64,2056]{2,1,0:T(8,128)(2,1)}, bf16[1,64,2056]{2,1,0:T(8,128)(2,1)}, ...) | async-done | bytes 4720656 | tf_op jit(solution)/shard_map/psum | solution.py:621
  688.7 3.5 maximum_convert_fusion
  692.2 2.3 maximum_convert_fusion.1
  (358 shorter events, 96.7 us)
Async XLA Ops:
  7.2 15.3 %copy-start.32 = (bf16[2,4,64,2048]{3,2,1,0:T(8,128)(2,1)S(1)}, bf16[2,4,64,2048]{3,2,1,0:T(8,128)(2,1)}, u32[]{:S(2)}) copy-start(bf16[2,4,64,2048]{3,2,1,0:T(8,128)(2,1)} %param.34) | copy-start | bytes 6291460
  7.2 60.3 %all-gather.4.cloned.1.call-start = ((), (), s32[]{:S(2)}) async-start(), calls=%async_computation.7 | async-start | bytes 5013504 | tf_op jit(solution)/shard_map/all_gather | solution.py:487
  18.0 22.9 %collective-permute-start.1 = (bf16[336,512]{1,0:T(8,128)(2,1)S(1)}, bf16[336,512]{1,0:T(8,128)(2,1)S(1)}, u32[]{:S(2)}, u32[]{:S(2)}) collective-permute-start(bf16[336,512]{1,0:T(8,128)(2,1)S(1)} %get-tuple-element.217), channel_id=1, source_target_pairs={{0,1},{1,0},{2,5},{3,4},{4,3},{5,2},{6,7},{7,6},{8,9},{9,8},{10,13... | collective-permute-start | bytes 1032200 | tf_op jit(solution)/shard_map/ppermute | solution.py:407
  21.1 19.8 %collective-permute-start = (bf16[336,512]{1,0:T(8,128)(2,1)S(1)}, bf16[336,512]{1,0:T(8,128)(2,1)}, u32[]{:S(2)}, u32[]{:S(2)}) collective-permute-start(bf16[336,512]{1,0:T(8,128)(2,1)S(1)} %get-tuple-element.218), channel_id=1, source_target_pairs={{0,0},{1,1},{2,4},{3,5},{4,2},{5,3},{6,6},{7,7},{8,8},{9,9},{10,12... | collective-permute-start | bytes 1032200 | tf_op jit(solution)/shard_map/ppermute | solution.py:407
  34.8 43.8 %all-to-all-start = ((bf16[8,2,65536]{2,1,0:T(2,128)(2,1)}), bf16[8,2,65536]{2,1,0:T(2,128)(2,1)S(1)}, u32[]{:S(2)}, u32[]{:S(2)}) async-start(bf16[8,2,65536]{2,1,0:T(2,128)(2,1)} %reshape.608), calls=%async_computation | async-start | bytes 4194304 | tf_op jit(solution)/shard_map/all_to_all | solution.py:497
  40.8 52.3 %all-gather.6.cloned.1.call-start = ((), (), s32[]{:S(2)}) async-start(), calls=%async_computation.8 | async-start | bytes 1966080 | tf_op jit(solution)/shard_map/all_gather | solution.py:507
  42.3 61.5 %copy-start.17 = (bf16[2,160,512]{2,1,0:T(8,128)(2,1)}, bf16[2,160,512]{2,1,0:T(8,128)(2,1)S(1)}, u32[]{:S(2)}) copy-start(bf16[2,160,512]{2,1,0:T(8,128)(2,1)S(1)} %get-tuple-element.206) | copy-start | bytes 983044
  42.3 31.0 %copy-start.66 = (f32[2,160]{1,0:T(2,128)}, f32[2,160]{1,0:T(2,128)S(1)}, u32[]{:S(2)}) copy-start(f32[2,160]{1,0:T(2,128)S(1)} %broadcast_multiply_fusion.12) | copy-start | bytes 3844
  42.6 30.7 %copy-start.76 = (f32[2,160]{1,0:T(2,128)}, f32[2,160]{1,0:T(2,128)S(1)}, u32[]{:S(2)}) copy-start(f32[2,160]{1,0:T(2,128)S(1)} %add_rsqrt_fusion.3) | copy-start | bytes 3844
  69.1 7.5 %copy-start.74 = (f32[512]{0:T(512)}, f32[512]{0:T(512)S(1)}, u32[]{:S(2)}) copy-start(f32[512]{0:T(512)S(1)} %get-tuple-element.196) | copy-start | bytes 6148
  69.2 36.5 %copy-start.68 = (f32[512]{0:T(512)}, f32[512]{0:T(512)S(1)}, u32[]{:S(2)}) copy-start(f32[512]{0:T(512)S(1)} %get-tuple-element.194) | copy-start | bytes 6148
  69.2 88.2 %copy-start.78 = (f32[512]{0:T(512)}, f32[512]{0:T(512)S(1)}, u32[]{:S(2)}) copy-start(f32[512]{0:T(512)S(1)} %get-tuple-element.192) | copy-start | bytes 6148
  69.2 88.2 %copy-start.86 = (f32[512]{0:T(512)}, f32[512]{0:T(512)S(1)}, u32[]{:S(2)}) copy-start(f32[512]{0:T(512)S(1)} %get-tuple-element.191) | copy-start | bytes 6148
  73.4 99.5 %all-gather.8.cloned.1.call-start = ((), (), s32[]{:S(2)}) async-start(), calls=%async_computation.9 | async-start | bytes 1966080 | tf_op jit(solution)/shard_map/all_gather | solution.py:507
  78.6 28.8 %copy-start.54 = (f32[320,4]{0,1:T(4,128)}, f32[320,4]{0,1:T(4,128)S(1)}, u32[]{:S(2)}) copy-start(f32[320,4]{0,1:T(4,128)S(1)} %squeeze.95) | copy-start | bytes 15364
  105.9 53.9 %copy-start.21 = (bf16[320,512]{1,0:T(8,128)(2,1)}, bf16[320,512]{1,0:T(8,128)(2,1)S(1)}, u32[]{:S(2)}) copy-start(bf16[320,512]{1,0:T(8,128)(2,1)S(1)} %add_convert_fusion.4) | copy-start | bytes 983044
  107.3 50.1 %copy-start.50 = (f32[320,4]{0,1:T(4,128)}, f32[320,4]{0,1:T(4,128)S(1)}, u32[]{:S(2)}) copy-start(f32[320,4]{0,1:T(4,128)S(1)} %get-tuple-element.238) | copy-start | bytes 15364
  107.3 52.6 %copy-start.58 = (f32[320]{0:T(512)}, f32[320]{0:T(512)S(1)}, u32[]{:S(2)}) copy-start(f32[320]{0:T(512)S(1)} %get-tuple-element.237) | copy-start | bytes 3844
  107.3 52.5 %copy-start.64 = (f32[320]{0:T(512)}, f32[320]{0:T(512)S(1)}, u32[]{:S(2)}) copy-start(f32[320]{0:T(512)S(1)} %fusion.48) | copy-start | bytes 3844
  161.7 140.8 %reduce-scatter.13.cloned.1.call-start = ((), (), s32[]{:S(2)}) async-start(), calls=%async_computation.12 | async-start | bytes 1966080
  180.7 45.7 %copy-start.34 = (bf16[8,64,320]{2,1,0:T(8,128)(2,1)}, bf16[8,64,320]{2,1,0:T(8,128)(2,1)S(1)}, u32[]{:S(2)}) copy-start(bf16[8,64,320]{2,1,0:T(8,128)(2,1)S(1)} %fusion.24) | copy-start | bytes 983044
  226.4 47.2 %copy-start.7 = (f32[320,512]{1,0:T(8,128)S(1)}, f32[320,512]{1,0:T(8,128)}, u32[]{:S(2)}) copy-start(f32[320,512]{1,0:T(8,128)} %copy-done.6) | copy-start | bytes 1966084
  226.4 49.7 %copy-start.27 = (bf16[2,160,512]{2,1,0:T(8,128)(2,1)S(1)}, bf16[2,160,512]{2,1,0:T(8,128)(2,1)}, u32[]{:S(2)}) copy-start(bf16[2,160,512]{2,1,0:T(8,128)(2,1)} %pad_maximum_fusion.11) | copy-start | bytes 983044
  293.6 10.4 %copy-start.73 = (f32[320]{0:T(512)S(1)}, f32[320]{0:T(512)}, u32[]{:S(2)}) copy-start(f32[320]{0:T(512)} %copy-done.72) | copy-start | bytes 3844
  293.6 10.4 %copy-start.79 = (f32[512]{0:T(512)S(1)}, f32[512]{0:T(512)}, u32[]{:S(2)}) copy-start(f32[512]{0:T(512)} %copy-done.78) | copy-start | bytes 6148
  293.6 10.5 %copy-start.81 = (f32[320]{0:T(512)S(1)}, f32[320]{0:T(512)}, u32[]{:S(2)}) copy-start(f32[320]{0:T(512)} %copy-done.80) | copy-start | bytes 3844
  293.6 100.7 %reduce-scatter.15.cloned.1.call-start = ((), (), s32[]{:S(2)}) async-start(), calls=%async_computation.13 | async-start | bytes 1966080
  308.4 46.0 %copy-start.51 = (f32[320,4]{0,1:T(4,128)S(1)}, f32[320,4]{0,1:T(4,128)}, u32[]{:S(2)}) copy-start(f32[320,4]{0,1:T(4,128)} %copy-done.50) | copy-start | bytes 15364
  308.4 46.0 %copy-start.55 = (f32[320,4]{0,1:T(4,128)S(1)}, f32[320,4]{0,1:T(4,128)}, u32[]{:S(2)}) copy-start(f32[320,4]{0,1:T(4,128)} %copy-done.54) | copy-start | bytes 15364
  308.4 46.0 %copy-start.59 = (f32[320]{0:T(512)S(1)}, f32[320]{0:T(512)}, u32[]{:S(2)}) copy-start(f32[320]{0:T(512)} %copy-done.58) | copy-start | bytes 3844
  308.4 46.0 %copy-start.65 = (f32[320]{0:T(512)S(1)}, f32[320]{0:T(512)}, u32[]{:S(2)}) copy-start(f32[320]{0:T(512)} %copy-done.64) | copy-start | bytes 3844
  308.4 47.5 %copy-start.9 = (f32[320,512]{1,0:T(8,128)S(1)}, f32[320,512]{1,0:T(8,128)}, u32[]{:S(2)}) copy-start(f32[320,512]{1,0:T(8,128)} %copy-done.8) | copy-start | bytes 1966084
  308.4 47.5 %copy-start.61 = (f32[320]{0:T(512)S(1)}, f32[320]{0:T(512)}, u32[]{:S(2)}) copy-start(f32[320]{0:T(512)} %copy-done.60) | copy-start | bytes 3844
  308.4 47.5 %copy-start.69 = (f32[512]{0:T(512)S(1)}, f32[512]{0:T(512)}, u32[]{:S(2)}) copy-start(f32[512]{0:T(512)} %copy-done.68) | copy-start | bytes 6148
  308.4 47.5 %copy-start.71 = (f32[320]{0:T(512)S(1)}, f32[320]{0:T(512)}, u32[]{:S(2)}) copy-start(f32[320]{0:T(512)} %copy-done.70) | copy-start | bytes 3844
  357.9 10.0 %slice-start = ((s8[6553600]{0:T(1024)(128)(4,1)}), s8[2359296]{0:T(1024)(128)(4,1)S(1)}, s32[]{:S(2)}) async-start(s8[6553600]{0:T(1024)(128)(4,1)} %bitcast.201), calls=%async_computation.15 | async-start | bytes 4718592
  375.9 80.2 %reduce-scatter.11.cloned.1.call-start = ((), (), s32[]{:S(2)}) async-start(), calls=%async_computation.11 | async-start | bytes 2506752 | tf_op jit(solution)/shard_map/reduce_scatter | solution.py:615
  385.3 112.3 %reduce-scatter.9.cloned.1.call-start = ((), (), s32[]{:S(2)}) async-start(), calls=%async_computation.10 | async-start | bytes 2506752 | tf_op jit(solution)/shard_map/reduce_scatter | solution.py:615
  408.8 23.6 %all-to-all-start.2 = ((bf16[4,512,256]{2,0,1:T(4,128)(2,1)}), bf16[4,512,256]{2,0,1:T(4,128)(2,1)S(1)}, u32[]{:S(2)}, u32[]{:S(2)}) async-start(bf16[4,512,256]{2,0,1:T(4,128)(2,1)} %bitcast.77), calls=%async_computation.4 | async-start | bytes 2097152 | tf_op jit(solution)/shard_map/all_to_all | solution.py:619
  432.4 21.8 %all-to-all-start.1 = ((bf16[4,512,256]{2,0,1:T(4,128)(2,1)}), bf16[4,512,256]{2,0,1:T(4,128)(2,1)S(1)}, u32[]{:S(2)}, u32[]{:S(2)}) async-start(bf16[4,512,256]{2,0,1:T(4,128)(2,1)} %bitcast.74), calls=%async_computation.3 | async-start | bytes 2097152 | tf_op jit(solution)/shard_map/all_to_all | solution.py:619
  436.0 246.6 %all-reduce.6.cloned.1.call-start = ((), (), s32[]{:S(2)}) async-start(), calls=%async_computation.14 | async-start | bytes 9502720 | tf_op jit(solution)/shard_map/psum | solution.py:621
  454.8 42.8 %copy-start.46 = (f32[320,512]{1,0:T(8,128)S(1)}, f32[320,512]{1,0:T(8,128)}, u32[]{:S(2)}) copy-start(f32[320,512]{1,0:T(8,128)} %get-tuple-element.88) | copy-start | bytes 1966084
  456.2 43.8 %copy-start.13 = (f32[320,512]{1,0:T(8,128)S(1)}, f32[320,512]{1,0:T(8,128)}, u32[]{:S(2)}) copy-start(f32[320,512]{1,0:T(8,128)} %copy-done.12) | copy-start | bytes 1966084
  456.2 43.8 %copy-start.45 = (f32[320,512]{1,0:T(8,128)S(1)}, f32[320,512]{1,0:T(8,128)}, u32[]{:S(2)}) copy-start(f32[320,512]{1,0:T(8,128)} %get-tuple-element.252) | copy-start | bytes 1966084
  497.7 5.9 collective-permute-start.3
  499.2 4.3 collective-permute-start.2
  500.3 6.5 collective-permute-start.5
  500.9 5.9 collective-permute-start.4
  (63 other events, 214.6 us)
Sparse Core Ops, SparseCore 0:
  13.3 54.2 all-gather.3
  73.5 16.6 all-gather.5
  161.9 10.9 all-gather.7
  293.8 8.7 reduce-scatter.12
  376.0 9.9 reduce-scatter.14
  389.8 56.3 reduce-scatter.10
  450.1 47.4 reduce-scatter.8
  500.4 182.1 all-reduce.5

commit v3 on v2

--- a/solution.py
+++ b/solution.py
@@ -25,14 +25,6 @@
         - jnp.mean(grad_unit, -1, keepdims=True)
         - unit * jnp.mean(grad_unit * unit, -1, keepdims=True)
     )
-
-
-def heads_of(values):
-    return values.reshape(values.shape[0], values.shape[1] // HEAD, HEAD)
-
-
-def mm(form, left, right):
-    return jnp.einsum(form, left, right, preferred_element_type=F32)
 
 
 MESH = pl.DeviceIdType.MESH
@@ -273,18 +265,22 @@
     )(message, middle, up, down)
 
 
-def experts_backward(grad, blocks, act, slope, up, down, size, experts):
+def experts_backward(grad, blocks, act, slope, up, down, size, experts, job):
     rows, width = grad.shape
     wide = up.shape[1]
     hid = wide // experts
     group = Group(size)
 
-    def kernel(
-        grad_ref, blocks_ref, act_ref, slope_ref, up_ref, down_ref,
-        out_ref, tail_ref, up_out, down_out, *scratch,
-    ):
-        slots, blocks, act, slope, weighed, scaled, pre, load_sem = scratch[:8]
-        scratch = scratch[8:]
+    def kernel(grad_ref, blocks_ref, act_ref, slope_ref, up_ref, down_ref, *rest):
+        stages = []
+        if job:
+            job_refs, rest = rest[:3], rest[3:]
+        (out_ref, tail_ref, up_out, down_out), rest = rest[:4], rest[4:]
+        if job:
+            stages = job.stages(job_refs, rest[:3], rest[-len(job.scratch_shapes) :])
+            rest = rest[3 : -len(job.scratch_shapes)]
+        slots, blocks, act, slope, weighed, scaled, pre, load_sem = rest[:8]
+        scratch = rest[8:]
 
         def loads(slot):
             two = lax.rem(slot, 2)
@@ -296,7 +292,7 @@
 
         for load in loads(0):
             load.start()
-        greet(group.peers())
+        job.greet() if job else greet(group.peers())
         slots[0] = grad_ref[...]
         lane = lax.broadcasted_iota(jnp.int32, (16, wide), 1) // hid
         pick = (lane == lax.broadcasted_iota(jnp.int32, (16, wide), 0)).astype(F32).astype(BF16)
@@ -321,6 +317,8 @@
                 weighed[:, cols] = (pull * value).astype(BF16)
                 scaled[place, cols] = (value * gate).astype(BF16)
                 pre[place, cols] = (pull * gate * slope[two, :, cols].astype(F32)).astype(BF16)
+            for at, stage in enumerate(stages[:-1]):
+                pl.when(slot == at)(stage)
             by_expert = dot(pick, weighed[...], ((1,), (1,)))[:8]
             if rows < width:
                 by_expert = jnp.concatenate([by_expert, jnp.zeros((8, width - rows), F32)], 1)
@@ -347,6 +345,8 @@
         group.collect(scratch, slots, rows, 16)
         out_ref[...] = scratch[0][0]
         tail_ref[...] = scratch[1][0, :8]
+        if job:
+            stages[-1]()
 
     return pl.pallas_call(
         kernel,
@@ -355,9 +355,11 @@
             jax.ShapeDtypeStruct((8, width), F32),
             jax.ShapeDtypeStruct((width, wide), BF16),
             jax.ShapeDtypeStruct((wide, width), BF16),
-        ),
-        in_specs=[in_vmem(), in_any(), in_any(), in_any(), in_vmem(), in_vmem()],
-        out_specs=(in_vmem(),) * 4,
+        )
+        + (job.out_shape if job else ()),
+        in_specs=[in_vmem(), in_any(), in_any(), in_any(), in_vmem(), in_vmem()]
+        + ([in_vmem()] * 3 if job else []),
+        out_specs=(in_vmem(),) * 4 + ((in_any(),) * 3 if job else ()),
         scratch_shapes=[
             pltpu.VMEM((size, rows, width), BF16),
             pltpu.VMEM((size, rows + META, width), BF16),
@@ -368,12 +370,526 @@
             pltpu.VMEM((size * rows, wide), BF16),
             pltpu.SemaphoreType.DMA((2, 3)),
         ]
-        + group.scratch(rows, 16, width),
+        + group.scratch(rows, 16, width)
+        + (job.scratch_shapes if job else []),
         compiler_params=pltpu.CompilerParams(
-            collective_id=2, has_side_effects=True, vmem_limit_bytes=VMEM_LIMIT
+            collective_id=4 if job else 2, has_side_effects=True, vmem_limit_bytes=VMEM_LIMIT
         ),
-        name="experts_backward",
-    )(grad, blocks, act, slope, up, down)
+        name="experts_backward_and_sums" if job else "experts_backward",
+    )(grad, blocks, act, slope, up, down, *(job.args if job else ()))
+
+
+class LineSums:
+    PAIRS = (("down", 0), ("down", 1), ("up", 0), ("up", 1), ("dense", 0))
+
+    def __init__(self, dp, up, down, dense):
+        self.dp = dp
+        self.args = (up, down, dense)
+        self.chunk = {
+            "up": (dp,) + up.shape[2:],
+            "down": down.shape[1:],
+            "dense": (dense.shape[2] // 2, dense.shape[3]),
+        }
+        self.half = {"up": 2, "down": 2, "dense": 1}
+        chips = dp // 2
+        whole = dense.shape[2:]
+        self.out_shape = tuple(
+            jax.ShapeDtypeStruct((2 * self.half[kind],) + self.chunk[kind], BF16)
+            for kind in ("up", "down", "dense")
+        )
+        self.boxes = []
+        for kind in ("up", "down", "dense"):
+            half, chunk = self.half[kind], self.chunk[kind]
+            self.boxes += [
+                pltpu.VMEM((2 * half,) + chunk, BF16),
+                pltpu.VMEM((half,) + chunk, BF16),
+                pltpu.VMEM((half,) + chunk, BF16),
+                pltpu.VMEM((2 * half,) + chunk, BF16),
+                pltpu.SemaphoreType.DMA((2, 2 * half)),
+                pltpu.SemaphoreType.DMA((2, half)),
+                pltpu.SemaphoreType.DMA((2, 2 * half)),
+                pltpu.SemaphoreType.DMA((half,)),
+            ]
+        self.scratch_shapes = self.boxes + [
+            pltpu.VMEM((2,) + self.chunk["up"], BF16),
+            pltpu.SemaphoreType.DMA((2, 2, dp)),
+            pltpu.VMEM((chips,) + whole, BF16),
+            pltpu.VMEM((chips,) + whole, BF16),
+            pltpu.VMEM((chips,) + whole, BF16),
+            pltpu.VMEM((2,) + self.chunk["dense"], BF16),
+            pltpu.SemaphoreType.DMA((2,)),
+            pltpu.SemaphoreType.DMA((2, chips)),
+            pltpu.SemaphoreType.DMA((3,)),
+        ]
+
+    def greet(self):
+        me, mine = lax.axis_index("dp"), lax.axis_index("seq")
+        barrier = pltpu.get_barrier_semaphore()
+        middle = (mine == 1) | (mine == 2)
+        for r in range(1, self.dp):
+            pl.semaphore_signal(barrier, inc=1, device_id={"dp": me ^ r}, device_id_type=MESH)
+        pl.semaphore_signal(
+            barrier, inc=1, device_id={"seq": jnp.where(middle, 3 - mine, 1 + mine // 2)}, device_id_type=MESH
+        )
+
+        @pl.when(middle)
+        def _():
+            pl.semaphore_signal(barrier, inc=1, device_id={"seq": 3 * (mine - 1)}, device_id_type=MESH)
+            pl.semaphore_wait(barrier, self.dp + 1)
+
+        @pl.when(jnp.logical_not(middle))
+        def _():
+            pl.semaphore_wait(barrier, self.dp)
+
+    def stages(self, refs, outs, scratch):
+        kinds = ("up", "down", "dense")
+        boxes = {kind: scratch[8 * at : 8 * at + 8] for at, kind in enumerate(kinds)}
+        up_mine, up_sem, near_got, near, far_got, dense_mine, near_sem, far_sem, out_sem = scratch[24:]
+        up, down, dense = refs
+        me, mine = lax.axis_index("dp"), lax.axis_index("seq")
+        core = lax.rem(me, 2)
+        next_core = {"dp": me ^ 1}
+        middle = (mine == 1) | (mine == 2)
+        at_end = jnp.logical_not(middle)
+        inner = {"seq": jnp.where(middle, 3 - mine, 1 + mine // 2)}
+        outer = {"seq": jnp.where(middle, 3 * (mine - 1), mine)}
+        owned = jnp.where(mine == 2, 1, 0)
+        chips = range(1, self.dp // 2)
+        spans = range(1, self.dp)
+
+        def source(kind, c):
+            return {"up": lambda: up.at[:, c], "down": lambda: down.at[c], "dense": lambda: dense_mine.at[c]}[
+                kind
+            ]()
+
+        def inward(kind, c):
+            box, sem = boxes[kind][0], boxes[kind][4]
+            return remote(source(kind, c), box.at[c], sem.at[0, c], sem.at[1, c], inner)
+
+        def across(kind, p):
+            sem = boxes[kind][5]
+            return remote(boxes[kind][2].at[p], boxes[kind][1].at[p], sem.at[0, p], sem.at[1, p], inner)
+
+        def outward(kind, c):
+            box, sem = boxes[kind][3], boxes[kind][6]
+            return remote(box.at[c], box.at[c], sem.at[0, c], sem.at[1, c], outer)
+
+        def between(kind, c, p):
+            box = boxes[kind][3]
+            return remote(box.at[c], box.at[c], boxes[kind][7].at[p], boxes[kind][6].at[1, c], inner)
+
+        def span(p, c, r):
+            return remote(
+                up_mine.at[p, me ^ r], boxes["up"][3].at[c, me], up_sem.at[0, p, r], up_sem.at[1, p, r],
+                {"dp": me ^ r},
+            )
+
+        def near_copy():
+            return remote(dense.at[:, 1 - core], near_got, near_sem.at[0], near_sem.at[1], next_core)
+
+        def far(m):
+            return remote(
+                near.at[(me // 2) ^ m], far_got.at[m], far_sem.at[0, m], far_sem.at[1, m], {"dp": me ^ (2 * m)}
+            )
+
+        def chunk_of(kind, p, own):
+            side = owned if own else 1 - owned
+            return p + side * self.half[kind]
+
+        def begin():
+            near_copy().start()
+
+            @pl.when(at_end)
+            def _():
+                for kind, p in self.PAIRS[:-1]:
+                    inward(kind, p).start()
+                    inward(kind, p + self.half[kind]).start()
+
+        def near_sum():
+            near_copy().wait_recv()
+            for at in range(self.dp // 2):
+                near[at] = (dense[at, core].astype(F32) + near_got[at].astype(F32)).astype(BF16)
+            for m in chips:
+                far(m).start()
+
+        def far_sum():
+            for m in chips:
+                far(m).wait_recv()
+            rows = self.chunk["dense"][0]
+            for at in range(2):
+                place = slice(at * rows, (at + 1) * rows)
+                total = near[me // 2, place].astype(F32)
+                for m in chips:
+                    total += far_got[m, place].astype(F32)
+                dense_mine[at] = total.astype(BF16)
+
+            @pl.when(at_end)
+            def _():
+                inward("dense", 0).start()
+                inward("dense", 1).start()
+
+        def relay(kind, p):
+            @pl.when(middle)
+            def _():
+                c = chunk_of(kind, p, False)
+                inward(kind, c).wait_recv()
+                boxes[kind][2][p] = (source(kind, c)[...].astype(F32) + boxes[kind][0][c].astype(F32)).astype(BF16)
+                across(kind, p).start()
+
+        def total(kind, p):
+            @pl.when(middle)
+            def _():
+                c = chunk_of(kind, p, True)
+                inward(kind, c).wait_recv()
+                across(kind, p).wait_recv()
+                whole = (
+                    source(kind, c)[...].astype(F32)
+                    + boxes[kind][0][c].astype(F32)
+                    + boxes[kind][1][p].astype(F32)
+                ).astype(BF16)
+                if kind == "up":
+                    up_mine[p] = whole
+                    boxes[kind][3][c, me] = up_mine[p, me]
+                    for r in spans:
+                        span(p, c, r).start()
+                else:
+                    boxes[kind][3][c] = whole
+                    between(kind, c, p).start()
+                    outward(kind, c).start()
+
+        def turn(p):
+            @pl.when(middle)
+            def _():
+                c = chunk_of("up", p, True)
+                for r in spans:
+                    span(p, c, r).wait_recv()
+                between("up", c, p).start()
+                outward("up", c).start()
+
+        def forward(kind, p):
+            @pl.when(middle)
+            def _():
+                c = chunk_of(kind, p, False)
+                outward(kind, c).wait_recv()
+                outward(kind, c).start()
+
+        def finish():
+            @pl.when(at_end)
+            def _():
+                for kind, p in self.PAIRS:
+                    outward(kind, p).wait_recv()
+                    outward(kind, p + self.half[kind]).wait_recv()
+                    inward(kind, p).wait_send()
+                    inward(kind, p + self.half[kind]).wait_send()
+
+            copies = [
+                pltpu.make_async_copy(boxes[kind][3], outs[at], out_sem.at[at]) for at, kind in enumerate(kinds)
+            ]
+            for copy in copies:
+                copy.start()
+
+            @pl.when(middle)
+            def _():
+                for kind, p in self.PAIRS:
+                    across(kind, p).wait_send()
+                    between(kind, chunk_of(kind, p, True), p).wait_send()
+                    outward(kind, p).wait_send()
+                    outward(kind, p + self.half[kind]).wait_send()
+                    if kind == "up":
+                        for r in spans:
+                            span(p, chunk_of(kind, p, True), r).wait_send()
+
+            near_copy().wait_send()
+            for m in chips:
+                far(m).wait_send()
+            for copy in copies:
+                copy.wait()
+
+        def both(*parts):
+            def stage():
+                for part, *of in parts:
+                    part(*of)
+
+            return stage
+
+        return [
+            begin,
+            both((near_sum,), (relay, "down", 0)),
+            both((total, "down", 0), (far_sum,)),
+            both((relay, "down", 1), (forward, "down", 0)),
+            both((total, "down", 1), (relay, "up", 0)),
+            both((total, "up", 0), (forward, "down", 1)),
+            both((relay, "up", 1), (turn, 0)),
+            both(
+                (total, "up", 1), (forward, "up", 0), (relay, "dense", 0), (turn, 1), (total, "dense", 0),
+                (forward, "up", 1), (forward, "dense", 0), (finish,),
+            ),
+        ]
+
+
+def sum_weights(job):
+    def kernel(*refs):
+        job.greet()
+        for stage in job.stages(refs[:3], refs[3:6], refs[6:]):
+            stage()
+
+    return pl.pallas_call(
+        kernel,
+        out_shape=job.out_shape,
+        in_specs=[in_vmem()] * 3,
+        out_specs=(in_any(),) * 3,
+        scratch_shapes=job.scratch_shapes,
+        compiler_params=pltpu.CompilerParams(
+            collective_id=3, has_side_effects=True, vmem_limit_bytes=VMEM_LIMIT
+        ),
+        name="sum_weights",
+    )(*job.args)
+
+
+def sum_weights_plainly(dp, up, down, dense):
+    dense = lax.psum_scatter(dense.reshape(dp, -1, dense.shape[-1]), "dp", scatter_dimension=0, tiled=True)
+    up = lax.all_to_all(up, "dp", split_axis=0, concat_axis=0, tiled=True)
+    return [lax.psum(jnp.swapaxes(up, 0, 1), "seq"), lax.psum(down, "seq"), lax.psum(dense, "seq")]
+
+
+NT = ((1,), (1,))
+TN = ((0,), (0,))
+
+
+def row_sums(values):
+    return jnp.sum(values, 0, keepdims=True)
+
+
+def pad_lanes(values, lanes):
+    if values.shape[1] == lanes:
+        return values
+    return jnp.concatenate([values, jnp.zeros((values.shape[0], lanes - values.shape[1]), values.dtype)], 1)
+
+
+def one_head(pair, parity):
+    lane = lax.broadcasted_iota(jnp.int32, pair.shape, 1) // HEAD
+    return jnp.where(lane == parity, pair.astype(F32), 0.0).astype(BF16)
+
+
+class Keys:
+    def __init__(self, share):
+        self.share = share
+
+    def peers(self):
+        me = lax.axis_index("dp")
+        return [{"dp": me ^ k} for k in range(1, self.share)]
+
+
+def attention_forward(state, proj_packed, proj_out, vectors, router, chosen, length, share):
+    rows, width = state.shape
+    keys_len = rows * share
+    heads = width // HEAD
+    experts = 4
+    keys = Keys(share)
+
+    def kernel(
+        state_ref, packed_ref, out_w_ref, vec_ref, router_ref, chosen_ref, length_ref,
+        message, middle, queries, kv, log_total, mixed, gates_ref,
+        all_kv, values_t, send, recv, save,
+    ):
+        me = lax.axis_index("dp")
+        part = lax.rem(me, share)
+        unit, _ = normalize(state_ref[...])
+        normed = (unit * vec_ref[0:1] + vec_ref[1:2]).astype(BF16)
+        all_kv[part] = dot(normed, packed_ref[:, width:]).astype(BF16)
+        greet(keys.peers())
+        copies = [
+            remote(all_kv.at[part], all_kv.at[part], send.at[k], recv.at[k], {"dp": me ^ k})
+            for k in range(1, share)
+        ]
+        for copy in copies:
+            copy.start()
+        queries[...] = (dot(normed, packed_ref[:, :width]) * HEAD ** (-0.5)).astype(BF16)
+        for copy in copies:
+            copy.wait()
+        saving = pltpu.make_async_copy(all_kv, kv, save)
+        saving.start()
+        for at in range(share):
+            values_t[:, at * rows : (at + 1) * rows] = jnp.transpose(
+                all_kv[at, :, width:].astype(F32)
+            ).astype(BF16)
+        valid = lax.broadcasted_iota(jnp.int32, (keys_len, rows), 0) < length_ref[0]
+
+        def pair_of_heads(pair, carry):
+            lanes = pl.ds(pl.multiple_of(pair * 128, 128), 128)
+            keys_pair = all_kv[:, :, lanes].reshape(keys_len, 128)
+            queries_pair = queries[:, lanes]
+            for parity in range(2):
+                head = 2 * pair + parity
+                scores = dot(keys_pair, one_head(queries_pair, parity), NT)
+                scores = jnp.where(valid, scores, NEG)
+                highest = jnp.max(scores, 0, keepdims=True)
+                expo = jnp.exp(scores - highest)
+                totals = row_sums(expo)
+                log_total[head] = highest + jnp.log(totals)
+                place = pl.ds(pl.multiple_of(head * HEAD, HEAD), HEAD)
+                mixed[place, :] = (dot(values_t[place, :], expo.astype(BF16)) / totals).astype(BF16)
+            return carry
+
+        lax.fori_loop(0, heads // 2, pair_of_heads, 0)
+        middle[...] = state_ref[...] + dot(mixed[...], out_w_ref[...], TN)
+        unit, _ = normalize(middle[...])
+        normed = (unit * vec_ref[2:3] + vec_ref[3:4]).astype(BF16)
+        message[:rows] = normed
+        logits = dot(router_ref[...], normed, NT)[:8]
+        row = lax.broadcasted_iota(jnp.int32, logits.shape, 0)
+        logits = jnp.where(row < experts, logits, NEG)
+        expo = jnp.exp(logits - jnp.max(logits, 0, keepdims=True))
+        gates = expo / row_sums(expo)
+        gates_ref[...] = gates
+        message[rows:] = split_rows(pad_lanes(gates * chosen_ref[...], width))
+        saving.wait()
+
+    return pl.pallas_call(
+        kernel,
+        out_shape=(
+            jax.ShapeDtypeStruct((rows + META, width), BF16),
+            jax.ShapeDtypeStruct((rows, width), F32),
+            jax.ShapeDtypeStruct((rows, width), BF16),
+            jax.ShapeDtypeStruct((share, rows, 2 * width), BF16),
+            jax.ShapeDtypeStruct((heads, 1, rows), F32),
+            jax.ShapeDtypeStruct((width, rows), BF16),
+            jax.ShapeDtypeStruct((8, rows), F32),
+        ),
+        in_specs=[in_vmem()] * 6 + [pl.BlockSpec(memory_space=pltpu.SMEM)],
+        out_specs=(in_vmem(),) * 3 + (in_any(),) + (in_vmem(),) * 3,
+        scratch_shapes=[
+            pltpu.VMEM((share, rows, 2 * width), BF16),
+            pltpu.VMEM((width, keys_len), BF16),
+            pltpu.SemaphoreType.DMA((share,)),
+            pltpu.SemaphoreType.DMA((share,)),
+            pltpu.SemaphoreType.DMA,
+        ],
+        compiler_params=pltpu.CompilerParams(
+            collective_id=5, has_side_effects=True, vmem_limit_bytes=VMEM_LIMIT
+        ),
+        name="attention_forward",
+    )(state, proj_packed, proj_out, vectors, router, chosen, length)
+
+
+def attention_backward(
+    grad, back, back_tail, state, middle, message, gates, chosen, queries, kv, log_total, mixed,
+    proj_packed, proj_out, vectors, router, length, share,
+):
+    rows, width = state.shape
+    keys_len = rows * share
+    heads = width // HEAD
+    columns = 4 * width + 128
+    keys = Keys(share)
+
+    def kernel(
+        grad_ref, back_ref, tail_ref, state_ref, mid_ref, msg_ref, gates_ref, chosen_ref, queries, kv,
+        log_total, mixed, packed_ref, out_w_ref, vec_ref, router_ref, length_ref,
+        new_ref, new_low_ref, dense,
+        keys_t, normed_ref, grad_mid, grad_heads, grad_q, kv_grads, kv_got, grad_packed, send, recv,
+    ):
+        me = lax.axis_index("dp")
+        part = lax.rem(me, share)
+        gates = gates_ref[...]
+        grad_gates = tail_ref[:, :rows] * chosen_ref[...]
+        grad_logits = split_rows(gates * (grad_gates - row_sums(gates * grad_gates)))
+        twice = jnp.concatenate([router_ref[:8].astype(F32)] * 2, 0).astype(BF16)
+        grad_normed = back_ref[...] + dot(grad_logits, twice, TN)
+        router_grad = dot(grad_logits, msg_ref[:rows])
+        router_grad = router_grad[:8] + router_grad[8:]
+        unit, inverse = normalize(mid_ref[...])
+        gain_two = row_sums(grad_normed * unit)
+        bias_two = row_sums(grad_normed)
+        grad_mid[...] = grad_ref[...] + norm_back(grad_normed * vec_ref[2:3], unit, inverse)
+        low = grad_mid[...].astype(BF16)
+        dense[:, 3 * width : 4 * width] = dot(mixed[...], low).astype(BF16)
+        grad_heads[...] = dot(low, out_w_ref[...], NT).astype(BF16)
+        for at in range(share):
+            keys_t[:, at * rows : (at + 1) * rows] = jnp.transpose(kv[at, :, :width].astype(F32)).astype(BF16)
+        valid = lax.broadcasted_iota(jnp.int32, (keys_len, rows), 0) < length_ref[0]
+
+        def pair_of_heads(pair, carry):
+            lanes = pl.ds(pl.multiple_of(pair * 128, 128), 128)
+            value_lanes = pl.ds(pl.multiple_of(width + pair * 128, 128), 128)
+            keys_pair = kv[:, :, lanes].reshape(keys_len, 128)
+            values_pair = kv[:, :, value_lanes].reshape(keys_len, 128)
+            grad_k = jnp.zeros((keys_len, 128), F32)
+            grad_v = jnp.zeros((keys_len, 128), F32)
+            for parity in range(2):
+                head = 2 * pair + parity
+                query = one_head(queries[:, lanes], parity)
+                pull = one_head(grad_heads[:, lanes], parity)
+                scores = dot(keys_pair, query, NT)
+                probs = jnp.where(valid, jnp.exp(scores - log_total[head]), 0.0)
+                grad_probs = dot(values_pair, pull, NT)
+                grad_scores = probs * (grad_probs - row_sums(probs * grad_probs))
+                grad_scores = grad_scores.astype(BF16)
+                grad_v += dot(probs.astype(BF16), pull)
+                grad_k += dot(grad_scores, query)
+                place = pl.ds(pl.multiple_of(head * HEAD, HEAD), HEAD)
+                grad_q[place, :] = dot(keys_t[place, :], grad_scores) * HEAD ** (-0.5)
+            kv_grads[:, :, lanes] = grad_k.astype(BF16).reshape(share, rows, 128)
+            kv_grads[:, :, value_lanes] = grad_v.astype(BF16).reshape(share, rows, 128)
+            return carry
+
+        lax.fori_loop(0, heads // 2, pair_of_heads, 0)
+        greet(keys.peers())
+        copies = [
+            remote(kv_grads.at[part ^ k], kv_got.at[k], send.at[k], recv.at[k], {"dp": me ^ k})
+            for k in range(1, share)
+        ]
+        for copy in copies:
+            copy.start()
+        unit, inverse = normalize(state_ref[...])
+        normed_ref[...] = (unit * vec_ref[0:1] + vec_ref[1:2]).astype(BF16)
+        grad_packed[:, :width] = jnp.transpose(grad_q[...]).astype(BF16)
+        for copy in copies:
+            copy.wait()
+        total = kv_grads[part].astype(F32)
+        for k in range(1, share):
+            total += kv_got[k].astype(F32)
+        grad_packed[:, width:] = total.astype(BF16)
+        grad_normed = dot(grad_packed[...], packed_ref[...], NT)
+        for block in range(3):
+            cols = slice(block * width, (block + 1) * width)
+            dense[:, cols] = dot(normed_ref[...], grad_packed[:, cols], TN).astype(BF16)
+        gain_one = row_sums(grad_normed * unit)
+        bias_one = row_sums(grad_normed)
+        new = grad_mid[...] + norm_back(grad_normed * vec_ref[0:1], unit, inverse)
+        new_ref[...] = new
+        new_low_ref[...] = new.astype(BF16)
+        tail = jnp.concatenate([gain_one, bias_one, gain_two, bias_two, router_grad[:4]], 0)
+        dense[:, 4 * width :] = pad_lanes(jnp.transpose(tail), 128).astype(BF16)
+
+    return pl.pallas_call(
+        kernel,
+        out_shape=(
+            jax.ShapeDtypeStruct((rows, width), F32),
+            jax.ShapeDtypeStruct((rows, width), BF16),
+            jax.ShapeDtypeStruct((width, columns), BF16),
+        ),
+        in_specs=[in_vmem()] * 16 + [pl.BlockSpec(memory_space=pltpu.SMEM)],
+        out_specs=(in_vmem(),) * 3,
+        scratch_shapes=[
+            pltpu.VMEM((width, keys_len), BF16),
+            pltpu.VMEM((rows, width), BF16),
+            pltpu.VMEM((rows, width), F32),
+            pltpu.VMEM((rows, width), BF16),
+            pltpu.VMEM((width, rows), F32),
+            pltpu.VMEM((share, rows, 2 * width), BF16),
+            pltpu.VMEM((share, rows, 2 * width), BF16),
+            pltpu.VMEM((rows, 3 * width), BF16),
+            pltpu.SemaphoreType.DMA((share,)),
+            pltpu.SemaphoreType.DMA((share,)),
+        ],
+        compiler_params=pltpu.CompilerParams(
+            collective_id=6, has_side_effects=True, vmem_limit_bytes=VMEM_LIMIT
+        ),
+        name="attention_backward",
+    )(
+        grad, back, back_tail, state, middle, message, gates, chosen, queries, kv, log_total, mixed,
+        proj_packed, proj_out, vectors, router, length,
+    )
 
 
 class Plan:
@@ -427,12 +943,6 @@
                 for local in range(self.images)
             ]
         )
-
-
-def attention_scores(queries, keys_all, length):
-    scores = mm("qhd,khd->hqk", heads_of(queries), heads_of(keys_all)) * HEAD ** (-0.5)
-    valid = jnp.arange(keys_all.shape[0]) < length
-    return jnp.where(valid[None, None, :], scores, NEG)
 
 
 def build(mesh):
@@ -476,12 +986,11 @@
         state = slots[:, :piece].reshape(rows, width).astype(F32)
         grad = slots[:, piece + META :].reshape(rows, width).astype(F32)
         meta = slots[:, piece : piece + META].astype(F32)
-        chosen_in = meta[:, : levels * experts, :piece]
-        chosen_in = jnp.transpose(
-            chosen_in.reshape(images, levels, experts, piece), (1, 0, 3, 2)
-        ).reshape(levels, rows, experts)
+        chosen_in = jnp.transpose(meta[:, : levels * experts, :piece], (1, 0, 2))
+        chosen_in = chosen_in.reshape(levels, experts, rows)
+        chosen_in = jnp.pad(chosen_in, ((0, 0), (0, 8 - experts), (0, 0)))
         length = meta[0, levels * experts, 0] * 4.0 + meta[0, levels * experts + 1, 0]
-        length = length.astype(jnp.int32)
+        length = length.astype(jnp.int32).reshape(1)
 
         vectors = jnp.stack([ln1_gain, ln1_bias, ln2_gain, ln2_bias], -1)
         dense = lax.all_gather(
@@ -492,140 +1001,60 @@
         )
         proj_packed_all = dense[..., : 3 * width]
         proj_out_all = dense[..., 3 * width : 4 * width]
-        vectors = jnp.swapaxes(dense[..., 4 * width : 4 * width + 4], 1, 2)
-        router_all = dense[..., 4 * width + 4 :]
+        tails = jnp.swapaxes(dense[..., 4 * width : 4 * width + 8], 1, 2)
+        vectors = tails[:, :4].astype(F32)
+        router_all = jnp.pad(tails[:, 4 : 4 + experts], ((0, 0), (0, 16 - experts), (0, 0)))
         up_all = lax.all_to_all(expert_in, "dp", split_axis=3, concat_axis=2, tiled=True)
         up_all = jnp.swapaxes(up_all, 1, 2).reshape(levels, width, wide)
         down_all = expert_out.reshape(levels, wide, width)
 
         saved = []
         for level in range(levels):
-            gain_one, bias_one, gain_two, bias_two = vectors[level]
-            unit_one, inverse_one = normalize(state)
-            normed = (unit_one * gain_one + bias_one).astype(BF16)
-            packed = mm("ld,de->le", normed, proj_packed_all[level]).astype(BF16)
-            keys_values = lax.all_gather(
-                packed[:, width:], "dp", axis=0, tiled=True, axis_index_groups=plan.groups
+            weights = (proj_packed_all[level], proj_out_all[level], vectors[level], router_all[level])
+            message, middle, queries, kv, log_total, mixed, gates = attention_forward(
+                state, *weights, chosen_in[level], length, plan.share
             )
-            queries = packed[:, :width]
-            keys_all, values_all = keys_values[:, :width], keys_values[:, width:]
-            scores = attention_scores(queries, keys_all, length)
-            highest = jnp.max(scores, -1, keepdims=True)
-            expo = jnp.exp(scores - highest)
-            totals = jnp.sum(expo, -1, keepdims=True)
-            log_total = highest + jnp.log(totals)
-            weights = (expo / totals).astype(BF16)
-            mixed = mm("hqk,khd->qhd", weights, heads_of(values_all)).reshape(rows, width).astype(BF16)
-            middle = state + mm("ld,de->le", mixed, proj_out_all[level])
-            unit_two, inverse_two = normalize(middle)
-            normed_two = (unit_two * gain_two + bias_two).astype(BF16)
-            logits = mm("ld,de->le", normed_two, router_all[level])
-            gates = jax.nn.softmax(logits, -1)
-            chosen = chosen_in[level]
-            combine = gates * chosen
-            gate_rows = jnp.zeros((8, width), F32).at[:experts, :rows].set(combine.T)
-            message = jnp.concatenate([normed_two, split_rows(gate_rows)], 0)
-            state, blocks, act, slope = experts_forward(
+            new_state, blocks, act, slope = experts_forward(
                 message, middle, up_all[level], down_all[level], plan.dp, experts
             )
-            saved.append(
-                dict(
-                    unit_one=unit_one,
-                    inverse_one=inverse_one,
-                    normed=normed,
-                    queries=queries,
-                    keys_all=keys_all,
-                    values_all=values_all,
-                    log_total=log_total,
-                    mixed=mixed,
-                    unit_two=unit_two,
-                    inverse_two=inverse_two,
-                    normed_two=normed_two,
-                    gates=gates,
-                    chosen=chosen,
-                    blocks=blocks,
-                    act=act,
-                    slope=slope,
-                )
+            attended = (
+                state, middle, message, gates, chosen_in[level], queries, kv, log_total, mixed
+            ) + weights
+            saved.append((attended, (blocks, act, slope)))
+            state = new_state
+        output = plan.to_pieces(state.astype(BF16).reshape(images, piece, width))
+
+        grads = [None] * levels
+        job = None
+        grad_low = grad.astype(BF16)
+        for level in reversed(range(levels)):
+            attended, routed = saved[level]
+            back, back_tail, up_grad, down_grad, *sums = experts_backward(
+                grad_low, *routed, up_all[level], down_all[level], plan.dp, experts, job
             )
-        output = plan.to_pieces(state.astype(BF16).reshape(images, piece, width))
-
-        grads = [None] * levels
-        for level in reversed(range(levels)):
-            kept = saved[level]
-            gain_one, bias_one, gain_two, bias_two = vectors[level]
-            back, back_tail, up_grad, down_grad = experts_backward(
-                grad.astype(BF16),
-                kept["blocks"],
-                kept["act"],
-                kept["slope"],
-                up_all[level],
-                down_all[level],
-                plan.dp,
-                experts,
+            if job:
+                grads[level + 1] = sums
+            grad, grad_low, dense_grad = attention_backward(
+                grad, back, back_tail, *attended, length, plan.share
             )
-            grad_combine = back_tail[:experts, :rows].T
-            gates = kept["gates"]
-            grad_gates = grad_combine * kept["chosen"]
-            grad_logits = gates * (grad_gates - jnp.sum(gates * grad_gates, -1, keepdims=True))
-            router = router_all[level].astype(F32)
-            back = back + jnp.dot(grad_logits, router.T, precision=lax.Precision.HIGHEST)
-            router_grad = jnp.dot(
-                kept["normed_two"].astype(F32).T, grad_logits, precision=lax.Precision.HIGHEST
+            strip = width // plan.dp // 4
+            weight_grads = (
+                up_grad.reshape(plan.dp, 4, strip, wide),
+                down_grad.reshape(4, wide // 4, width),
+                dense_grad.reshape(plan.dp // 2, 2, width // plan.dp, -1),
             )
-            unit_two = kept["unit_two"]
-            gain_two_grad = jnp.sum(back * unit_two, 0)
-            bias_two_grad = jnp.sum(back, 0)
-            grad_middle = grad + norm_back(back * gain_two, unit_two, kept["inverse_two"])
-            grad_branch = grad_middle.astype(BF16)
-            out_grad = mm("ld,le->de", kept["mixed"], grad_branch)
-            grad_mixed = mm("le,de->ld", grad_branch, proj_out_all[level]).astype(BF16)
-            queries, keys_all, values_all = kept["queries"], kept["keys_all"], kept["values_all"]
-            probs = jnp.exp(attention_scores(queries, keys_all, length) - kept["log_total"])
-            grad_split = heads_of(grad_mixed)
-            grad_v = mm("hqk,qhd->khd", probs.astype(BF16), grad_split)
-            grad_probs = mm("qhd,khd->hqk", grad_split, heads_of(values_all))
-            grad_scores = (
-                probs * (grad_probs - jnp.sum(probs * grad_probs, -1, keepdims=True))
-            ).astype(BF16)
-            scale = HEAD ** (-0.5)
-            grad_q = scale * mm("hqk,khd->qhd", grad_scores, heads_of(keys_all))
-            grad_k = scale * mm("hqk,qhd->khd", grad_scores, heads_of(queries))
-            grad_kv = jnp.concatenate(
-                [grad_k.reshape(length_all, width), grad_v.reshape(length_all, width)], -1
-            )
-            grad_kv = lax.psum_scatter(
-                grad_kv.astype(BF16),
-                "dp",
-                scatter_dimension=0,
-                tiled=True,
-                axis_index_groups=plan.groups,
-            )
-            grad_packed = jnp.concatenate([grad_q.reshape(rows, width).astype(BF16), grad_kv], -1)
-            back_one = mm("le,de->ld", grad_packed, proj_packed_all[level])
-            packed_grad = mm("ld,le->de", kept["normed"], grad_packed)
-            unit_one = kept["unit_one"]
-            gain_one_grad = jnp.sum(back_one * unit_one, 0)
-            bias_one_grad = jnp.sum(back_one, 0)
-            grad = grad_middle + norm_back(back_one * gain_one, unit_one, kept["inverse_one"])
-            vector_grads = jnp.stack(
-                [gain_one_grad, bias_one_grad, gain_two_grad, bias_two_grad], -1
-            )
-            dense_grad = jnp.concatenate([packed_grad, out_grad, vector_grads, router_grad], -1)
-            dense_grad = lax.psum_scatter(
-                dense_grad.astype(BF16), "dp", scatter_dimension=0, tiled=True
-            )
-            up_grad = jnp.swapaxes(up_grad.astype(BF16).reshape(width, experts, slice_hid), 0, 1)
-            up_grad = lax.all_to_all(up_grad, "dp", split_axis=1, concat_axis=2, tiled=True)
-            grads[level] = (
-                lax.psum(dense_grad, "seq").astype(F32),
-                lax.psum(up_grad, "seq").astype(F32),
-                lax.psum(
-                    down_grad.astype(BF16).reshape(experts, slice_hid, width), "seq"
-                ).astype(F32),
-            )
-        token_grad = plan.to_pieces(grad.astype(BF16).reshape(images, piece, width)).astype(F32)
-        dense_grad, up_grad, down_grad = (jnp.stack(items) for items in zip(*grads))
+            if plan.seq == 4:
+                job = LineSums(plan.dp, *weight_grads)
+            else:
+                grads[level] = sum_weights_plainly(plan.dp, *weight_grads)
+        if job:
+            grads[0] = sum_weights(job)
+        token_grad = plan.to_pieces(grad_low.reshape(images, piece, width)).astype(F32)
+        up_grad, down_grad, dense_grad = (jnp.stack(items).astype(F32) for items in zip(*grads))
+        up_grad = up_grad.reshape(levels, 4, plan.dp, strip, experts, slice_hid)
+        up_grad = jnp.transpose(up_grad, (0, 4, 1, 3, 2, 5)).reshape(expert_in.shape)
+        down_grad = down_grad.reshape(expert_out.shape)
+        dense_grad = dense_grad.reshape(levels, width // plan.dp, -1)
         vector_grads = dense_grad[..., 4 * width : 4 * width + 4]
         return (
             output,
@@ -636,7 +1065,7 @@
             dense_grad[..., 3 * width : 4 * width],
             vector_grads[..., 2],
             vector_grads[..., 3],
-            dense_grad[..., 4 * width + 4 :],
+            dense_grad[..., 4 * width + 4 : 4 * width + 4 + experts],
             up_grad,
             down_grad,
         )

time: 708 us -> 540 us (0.76)
  waiting for transfers between devices: 293 us -> 24.3 us
  Pallas kernels: 180 us -> 382 us
  matrix products: 60.8 us -> 0 us
  other arithmetic: 39 us -> 12.9 us
  local copies, waits for them, and re-layouts: 89.8 us -> 80.2 us
  starting transfers between devices: 22.1 us -> 15 us
    psum x1 -> x0, waiting for transfers between devices: 174 us -> none  [shards(): lax.psum(dense_grad, 'seq').astype(F32)]
    pallas_call x0 -> x5, Pallas kernels: none -> 143 us  [the longest x1 86.2 us: sum_weights(): pl.pallas_call(kernel, out_shape=job.out_shape, in_specs=[in_vmem()] * 3,...]
    pallas_call x2, Pallas kernels: 91.6 us -> 157 us  [experts_backward(): pl.pallas_call(kernel, out_shape=(jax.ShapeDtypeStruct((rows, width), F32...]
    dot_general x30 -> x0, matrix products: 60.8 us -> none  [the longest x26 54.5 us: mm(): return jnp.einsum(form, left, right, preferred_element_type=F32)]
    reduce_scatter x2 -> x0, waiting for transfers between devices: 41.4 us -> none  [shards(): lax.psum_scatter(dense_grad.astype(BF16), 'dp', scatter_dimension=0, tile...]
    all_to_all x2 -> x0, waiting for transfers between devices: 32.4 us -> none  [shards(): lax.all_to_all(up_grad, 'dp', split_axis=1, concat_axis=2, tiled=True)]
    all_gather x1, waiting for transfers between devices: 24.9 us -> 0.01 us  [shards(): lax.all_gather(jnp.concatenate([qkv_weight, out_weight, vectors, router_w...]
    all_to_all x1, waiting for transfers between devices: 0.01 us -> 18.5 us  [shards(): lax.all_to_all(expert_in, 'dp', split_axis=3, concat_axis=2, tiled=True)]
  transfers between devices with their start and end apart: 17 -> 8, of which waited for: 9 -> 2; matrix products, arithmetic and copies ran while one was open for 13% -> 10% of each run, Pallas kernels for 0% -> 0%
where the time goes in v3:
time: 540 us; the launch traced here: 531 us
  Pallas kernels  382 us (71%)
  local copies, waits for them, and re-layouts  80.2 us (15%)
  waiting for transfers between devices  24.3 us (4%)
  between operations  16.2 us (3%)
  starting transfers between devices  15 us (3%)
  other arithmetic  12.9 us (2%)
    pallas_call x2, Pallas kernels, experts_backward(): pl.pallas_call(kernel, out_shape=(jax.ShapeDtypeStruct((rows, width), F32...  157 us
    pallas_call x1, Pallas kernels, sum_weights(): pl.pallas_call(kernel, out_shape=job.out_shape, in_specs=[in_vmem()] * 3,...  86.2 us
    pallas_call x2, Pallas kernels, experts_forward(): pl.pallas_call(kernel, out_shape=(jax.ShapeDtypeStruct((rows, width), F32...  82.2 us
    pallas_call x2, Pallas kernels, attention_backward(): pl.pallas_call(kernel, out_shape=(jax.ShapeDtypeStruct((rows, width), F32...  33.5 us
    unnamed x39, local copies, waits for them, and re-layouts  32.3 us
    pallas_call x2, Pallas kernels, attention_forward(): pl.pallas_call(kernel, out_shape=(jax.ShapeDtypeStruct((rows + META, widt...  23.7 us
    all_to_all x1, waiting for transfers between devices, shards(): lax.all_to_all(expert_in, 'dp', split_axis=3, concat_axis=2, tiled=True)  18.5 us
  transfers between devices with their start and end apart: 8, of which 2 were waited for; matrix products, arithmetic and copies ran while one was open for 10% of the time, Pallas kernels for 0%

profile of v3, /device:TPU:0, one launch (start us, length us, event | category | flops | bytes accessed | tf_op | source)
XLA Modules:
  0.0 530.7 jit_solution(10732577330530188758)
XLA Ops:
  7.2 1.5 copy.124
  8.8 1.0 copy.125
  13.7 3.3 concatenate.17
  17.1 4.8 copy.135
  21.9 7.6 %reshape.258 = bf16[8,2,65536]{2,1,0:T(2,128)(2,1)} reshape(bf16[2048,2,4,64]{3,2,1,0:T(4,128)(2,1)} %bitcast.99) | data formatting | bytes 4194304
  29.5 5.3 %all-to-all-start = ((bf16[8,2,65536]{2,1,0:T(2,128)(2,1)}), bf16[8,2,65536]{2,1,0:T(2,128)(2,1)S(1)}, u32[]{:S(2)}, u32[]{:S(2)}) async-start(bf16[8,2,65536]{2,1,0:T(2,128)(2,1)} %reshape.258), calls=%async_computation | async-start | bytes 4194304 | tf_op jit(solution)/shard_map/all_to_all | solution.py:1007
  36.3 1.6 collective-permute-start
  38.0 1.6 collective-permute-start.1
  39.6 3.1 fusion.18
  42.6 5.7 %collective-permute-done.1 = bf16[336,512]{1,0:T(8,128)(2,1)S(1)} collective-permute-done((bf16[336,512]{1,0:T(8,128)(2,1)S(1)}, bf16[336,512]{1,0:T(8,128)(2,1)S(1)}, u32[]{:S(2)}, u32[]{:S(2)}) %collective-permute-start.1) | collective-permute-done | bytes 344096 | tf_op jit(solution)/shard_map/ppermute | solution.py:923
  49.1 1.2 fusion
  52.9 1.0 bitcast_convert_fusion.state_ref
  53.9 0.9 bitcast_convert_fusion.1.grad_ref
  54.9 18.5 %all-to-all-done = bf16[8,2,65536]{2,1,0:T(2,128)(2,1)S(1)} async-done(((bf16[8,2,65536]{2,1,0:T(2,128)(2,1)}), bf16[8,2,65536]{2,1,0:T(2,128)(2,1)S(1)}, u32[]{:S(2)}, u32[]{:S(2)}) %all-to-all-start) | async-done | bytes 2097184 | tf_op jit(solution)/shard_map/all_to_all | solution.py:1007
  73.4 5.4 %reshape.259 = bf16[2048,2,4,64]{3,2,1,0:T(4,128)(2,1)} reshape(bf16[8,2,65536]{2,1,0:T(2,128)(2,1)S(1)} %all-to-all-done) | data formatting | bytes 4194304
  78.8 6.2 %copy.136 = bf16[2,4,8,64,256]{4,1,3,2,0:T(4,128)(2,1)S(1)} copy(bf16[2,4,8,64,256]{3,1,0,4,2:T(4,128)(2,1)} %bitcast.98) | data formatting | bytes 4194304 | tf_op jit(solution)/shard_map/all_to_all | solution.py:1007
  85.7 1.2 copy.149
  86.9 1.2 copy.150
  88.1 1.1 slice.214
  90.6 7.6 %fusion.17 = (bf16[1,512,1536]{2,0,1:T(2,128)(2,1)S(1)}, bf16[1,512,1536]{2,0,1:T(2,128)(2,1)S(1)}) fusion(bf16[2,512,2056]{2,0,1:T(2,128)(2,1)} %all-gather.2.cloned.1.call-done), kind=kLoop, calls=%fused_computation.76 | loop fusion | bytes 6291456 | tf_op jit(solution)/shard_map/slice | solution.py:1013
  98.2 1.5 copy.156
  99.7 3.1 fusion.16
  102.8 0.9 copy.158
  103.7 1.5 copy.155
  105.2 1.0 copy.157
  106.1 11.8 %attention_forward.2 = (bf16[336,512]{1,0:T(8,128)(2,1)}, f32[320,512]{1,0:T(8,128)}, bf16[320,512]{1,0:T(8,128)(2,1)}, bf16[2,320,1024]{2,1,0:T(8,128)(2,1)}, f...) custom-call(f32[320,512]{1,0:T(8,128)} %bitcast_convert_fusion.state_ref, ...), custom_call_target="tpu_custom_call" | custom-call | tf_op jit(solution)/shard_map/attention_forward/pallas_call | solution.py:748
  117.9 41.1 %experts_forward.2 = (f32[320,512]{1,0:T(8,128)}, bf16[8,336,512]{2,1,0:T(8,128)(2,1)}, bf16[8,320,1024]{2,1,0:T(8,128)(2,1)}, bf16[8,320,1024]{2,1,0:T(8,128)(2,1)}) custom-call(bf16[336,512]{1,0:T(8,128)(2,1)} %get-tuple-element.88.msg_ref, f32[320,512]{1,0:T(8,128)} %get-tuple-element.89.mid_ref, bf16[512,1024]{1,0:T(8,128)(2,1)} %bitcast.104, ...), custom_call_target="tpu_custom_call" | custom-call | tf_op jit(solution)/shard_map/experts_forward/pallas_call | solution.py:243
  159.0 11.9 %attention_forward.3 = (bf16[336,512]{1,0:T(8,128)(2,1)}, f32[320,512]{1,0:T(8,128)}, bf16[320,512]{1,0:T(8,128)(2,1)}, bf16[2,320,1024]{2,1,0:T(8,128)(2,1)}, f...) custom-call(f32[320,512]{1,0:T(8,128)} %get-tuple-element.90.state_ref, ...), custom_call_target="tpu_custom_call" | custom-call | tf_op jit(solution)/shard_map/attention_forward/pallas_call | solution.py:748
  171.0 41.1 %experts_forward.3 = (f32[320,512]{1,0:T(8,128)}, bf16[8,336,512]{2,1,0:T(8,128)(2,1)}, bf16[8,320,1024]{2,1,0:T(8,128)(2,1)}, bf16[8,320,1024]{2,1,0:T(8,128)(2,1)}) custom-call(bf16[336,512]{1,0:T(8,128)(2,1)} %get-tuple-element.91.msg_ref, f32[320,512]{1,0:T(8,128)} %get-tuple-element.92.mid_ref, bf16[512,1024]{1,0:T(8,128)(2,1)} %bitcast.108, ...), custom_call_target="tpu_custom_call" | custom-call | tf_op jit(solution)/shard_map/experts_forward/pallas_call | solution.py:243
  212.1 44.7 %experts_backward.1 = (f32[320,512]{1,0:T(8,128)}, f32[8,512]{1,0:T(8,128)}, bf16[512,1024]{1,0:T(8,128)(2,1)}, bf16[1024,512]{1,0:T(8,128)(2,1)}) custom-call(bf16[320,512]{1,0:T(8,128)(2,1)} %bitcast.119, bf16[8,336,512]{2,1,0:T(8,128)(2,1)} %get-tuple-element.94.blocks_ref, bf16[8,320,1024]{2,1,0:T(8,128)(2,1)} %get-tuple-element.95.act_ref, ...), custom_call_target="tpu_custom_call" | custom-call | tf_op jit(solution)/shard_map/experts_backward/pallas_call | solution.py:351
  256.7 16.8 %attention_backward.2 = (f32[320,512]{1,0:T(8,128)}, bf16[320,512]{1,0:T(8,128)(2,1)}, bf16[512,2176]{1,0:T(8,128)(2,1)}) custom-call(f32[320,512]{1,0:T(8,128)} %bitcast_convert_fusion.1.grad_ref, f32[320,512]{1,0:T(8,128)} %get-tuple-element.97.back_ref, f32[8,512]{1,0:T(8,128)} %get-tuple-element.98.tail_ref, f32[320,512]{1,0:T(8,128)} %get-tuple-element.90.state_ref, ...), custom_call_target="tpu_custom_call" | custom-call | tf_op jit(solution)/shard_map/attention_backward/pallas_call | solution.py:864
  273.5 111.9 %experts_backward_and_sums.1 = (f32[320,512]{1,0:T(8,128)}, f32[8,512]{1,0:T(8,128)}, bf16[512,1024]{1,0:T(8,128)(2,1)}, bf16[1024,512]{1,0:T(8,128)(2,1)}, bf16...) custom-call(bf16[320,512]{1,0:T(8,128)(2,1)} %get-tuple-element.105.grad_ref, ...), custom_call_target="tpu_custom_call" | custom-call | tf_op jit(solution)/shard_map/experts_backward_and_sums/pallas_call | solution.py:351
  385.4 16.7 %attention_backward.3 = (f32[320,512]{1,0:T(8,128)}, bf16[320,512]{1,0:T(8,128)(2,1)}, bf16[512,2176]{1,0:T(8,128)(2,1)}) custom-call(f32[320,512]{1,0:T(8,128)} %get-tuple-element.104.grad_ref, f32[320,512]{1,0:T(8,128)} %get-tuple-element.112.back_ref, f32[8,512]{1,0:T(8,128)} %get-tuple-element.113.tail_ref, f32[320,512]{1,0:T(8,128)} %bitcast_convert_fusion.state_ref, ...), custom_call_target="tpu_custom_call" | custom-call | tf_op jit(solution)/shard_map/attention_backward/pallas_call | solution.py:864
  402.1 86.2 %sum_weights.1 = (bf16[4,8,16,1024]{3,2,1,0:T(8,128)(2,1)}, bf16[4,256,512]{2,1,0:T(8,128)(2,1)}, bf16[2,32,2176]{2,1,0:T(8,128)(2,1)}) custom-call(bf16[8,4,16,1024]{3,2,1,0:T(8,128)(2,1)} %bitcast.127, bf16[4,256,512]{2,1,0:T(8,128)(2,1)} %bitcast.128, bf16[4,2,64,2176]{3,2,1,0:T(8,128)(2,1)} %bitcast.121), custom_call_target="tpu_custom_call" | custom-call | tf_op jit(solution)/shard_map/sum_weights/pallas_call | solution.py:636
  488.3 1.9 stack.100
  491.1 1.3 copy.139
  492.4 1.3 copy.140
  494.5 1.6 collective-permute-start.4
  496.0 1.1 convert_element_type.74
  497.9 2.9 collective-permute-start.2
  500.8 2.0 collective-permute-start.3
  502.8 2.3 maximum_convert_fusion
  505.1 1.3 convert_bitcast_fusion
  508.2 4.4 copy.141
  512.6 5.0 reshape.255
  517.6 1.3 copy.142
  518.9 0.9 copy.143
  520.4 1.3 fusion.4
  (75 shorter events, 15.7 us)
Async XLA Ops:
  7.2 9.9 %copy-start.2 = (bf16[2,4,64,2048]{3,2,1,0:T(8,128)(2,1)S(1)}, bf16[2,4,64,2048]{3,2,1,0:T(8,128)(2,1)}, u32[]{:S(2)}) copy-start(bf16[2,4,64,2048]{3,2,1,0:T(8,128)(2,1)} %param.30) | copy-start | bytes 6291460
  7.2 81.0 %all-gather.2.cloned.1.call-start = ((), (), s32[]{:S(2)}) async-start(), calls=%async_computation.1 | async-start | bytes 5013504 | tf_op jit(solution)/shard_map/all_gather | solution.py:996
  29.5 5.3 %copy-start.10 = (s32[2,640]{1,0:T(2,128)S(1)}, s32[2,640]{1,0:T(2,128)}, u32[]{:S(2)}) copy-start(s32[2,640]{1,0:T(2,128)} %param.22) | copy-start | bytes 15364
  29.5 5.6 %copy-start.11 = (s32[2,2,160,2]{2,3,1,0:T(2,128)S(1)}, s32[2,2,160,2]{2,3,1,0:T(2,128)}, u32[]{:S(2)}) copy-start(s32[2,2,160,2]{2,3,1,0:T(2,128)} %param.21) | copy-start | bytes 15364
  29.5 5.9 %copy-start.7 = (bf16[2,160,512]{2,1,0:T(8,128)(2,1)S(1)}, bf16[2,160,512]{2,1,0:T(8,128)(2,1)}, u32[]{:S(2)}) copy-start(bf16[2,160,512]{2,1,0:T(8,128)(2,1)} %param.20) | copy-start | bytes 983044
  29.5 6.0 %copy-start.9 = (bf16[2,160,512]{2,1,0:T(8,128)(2,1)S(1)}, bf16[2,160,512]{2,1,0:T(8,128)(2,1)}, u32[]{:S(2)}) copy-start(bf16[2,160,512]{2,1,0:T(8,128)(2,1)} %param.19) | copy-start | bytes 983044
  29.5 43.9 %all-to-all-start = ((bf16[8,2,65536]{2,1,0:T(2,128)(2,1)}), bf16[8,2,65536]{2,1,0:T(2,128)(2,1)S(1)}, u32[]{:S(2)}, u32[]{:S(2)}) async-start(bf16[8,2,65536]{2,1,0:T(2,128)(2,1)} %reshape.258), calls=%async_computation | async-start | bytes 4194304 | tf_op jit(solution)/shard_map/all_to_all | solution.py:1007
  36.3 6.3 %collective-permute-start = (bf16[336,512]{1,0:T(8,128)(2,1)}, bf16[336,512]{1,0:T(8,128)(2,1)S(1)}, u32[]{:S(2)}, u32[]{:S(2)}) collective-permute-start(bf16[336,512]{1,0:T(8,128)(2,1)} %get-tuple-element.201), channel_id=1, source_target_pairs={{0,0},{1,1},{2,4},{3,5},{4,2},{5,3},{6,6},{7,7},{8,8},{9,9},{10,12... | collective-permute-start | bytes 1032200 | tf_op jit(solution)/shard_map/ppermute | solution.py:923
  38.0 10.4 %collective-permute-start.1 = (bf16[336,512]{1,0:T(8,128)(2,1)S(1)}, bf16[336,512]{1,0:T(8,128)(2,1)S(1)}, u32[]{:S(2)}, u32[]{:S(2)}) collective-permute-start(bf16[336,512]{1,0:T(8,128)(2,1)S(1)} %get-tuple-element.200), channel_id=1, source_target_pairs={{0,1},{1,0},{2,5},{3,4},{4,3},{5,2},{6,7},{7,6},{8,9},{9,8},{10,13... | collective-permute-start | bytes 1032200 | tf_op jit(solution)/shard_map/ppermute | solution.py:923
  48.4 0.7 copy-start.6
  52.9 25.8 %copy-start.1 = (bf16[2,160,512]{2,1,0:T(8,128)(2,1)}, bf16[2,160,512]{2,1,0:T(8,128)(2,1)S(1)}, u32[]{:S(2)}) copy-start(bf16[2,160,512]{2,1,0:T(8,128)(2,1)S(1)} %get-tuple-element.196) | copy-start | bytes 983044
  488.3 2.0 copy-start.3
  490.3 3.4 copy-start.8
  493.7 9.1 %copy-start.4 = (bf16[4,256,512]{2,1,0:T(8,128)(2,1)S(1)}, bf16[4,256,512]{2,1,0:T(8,128)(2,1)}, u32[]{:S(2)}) copy-start(bf16[4,256,512]{2,1,0:T(8,128)(2,1)} %get-tuple-element.128) | copy-start | bytes 3145732
  493.7 9.1 %copy-start.5 = (bf16[4,256,512]{2,1,0:T(8,128)(2,1)S(1)}, bf16[4,256,512]{2,1,0:T(8,128)(2,1)}, u32[]{:S(2)}) copy-start(bf16[4,256,512]{2,1,0:T(8,128)(2,1)} %get-tuple-element.127) | copy-start | bytes 3145732
  494.5 25.9 %collective-permute-start.4 = (bf16[160,512]{1,0:T(8,128)(2,1)}, bf16[160,512]{1,0:T(8,128)(2,1)S(1)}, u32[]{:S(2)}, u32[]{:S(2)}) collective-permute-start(bf16[160,512]{1,0:T(8,128)(2,1)} %get-tuple-element.205), channel_id=1, source_target_pairs={{0,0},{1,1},{4,2},{5,3},{2,4},{3,5},{6,6},{7,7},{8,8},{9,9},{12,10... | collective-permute-start | bytes 491528 | tf_op jit(solution)/shard_map/ppermute | solution.py:938
  496.0 24.4 %collective-permute-start.5 = (bf16[160,512]{1,0:T(8,128)(2,1)}, bf16[160,512]{1,0:T(8,128)(2,1)}, u32[]{:S(2)}, u32[]{:S(2)}) collective-permute-start(bf16[160,512]{1,0:T(8,128)(2,1)} %get-tuple-element.204), channel_id=1, source_target_pairs={{1,0},{0,1},{5,2},{4,3},{3,4},{2,5},{7,6},{6,7},{9,8},{8,9},{13,10... | collective-permute-start | bytes 491528 | tf_op jit(solution)/shard_map/ppermute | solution.py:938
  497.9 22.5 %collective-permute-start.2 = (bf16[160,512]{1,0:T(8,128)(2,1)}, bf16[160,512]{1,0:T(8,128)(2,1)}, u32[]{:S(2)}, u32[]{:S(2)}) collective-permute-start(bf16[160,512]{1,0:T(8,128)(2,1)} %get-tuple-element.209), channel_id=1, source_target_pairs={{0,0},{1,1},{4,2},{5,3},{2,4},{3,5},{6,6},{7,7},{8,8},{9,9},{12,10... | collective-permute-start | bytes 491528 | tf_op jit(solution)/shard_map/ppermute | solution.py:938
  500.8 19.6 %collective-permute-start.3 = (bf16[160,512]{1,0:T(8,128)(2,1)}, bf16[160,512]{1,0:T(8,128)(2,1)}, u32[]{:S(2)}, u32[]{:S(2)}) collective-permute-start(bf16[160,512]{1,0:T(8,128)(2,1)} %get-tuple-element.208), channel_id=1, source_target_pairs={{1,0},{0,1},{5,2},{4,3},{3,4},{2,5},{7,6},{6,7},{9,8},{8,9},{13,10... | collective-permute-start | bytes 491528 | tf_op jit(solution)/shard_map/ppermute | solution.py:938
  506.8 1.4 copy-start
  512.6 5.0 slice-start
  517.6 1.3 slice-start.1
Sparse Core Ops, SparseCore 0:
  17.2 52.3 all-gather.1
